TPU v7x, 32 devices: a whole 2x2x4 slice. The times are simulated.
32 devices in a mesh: dp: 8 (over y, x, core), seq: 4 (over z).
Axes of the slice: x: 2, y: 2, z: 4, core: 2. Of those that a mesh axis runs over, the one named last changes fastest.
Arguments:
- tokens: bfloat16 [64, 512, 768], P('dp', 'seq'), may hold values from -6 to 6
- cotangent: bfloat16 [64, 512, 768], P('dp', 'seq'), may hold values from -6 to 6
- lengths: int32 [64], P('dp'), may hold values from 64 to 512, as said below
- owner: int32 [72], replicated, may hold values from 0 to 143, as said below
- master: float32 [144, 128, 768], P('dp'), as said below
- moment: float32 [144, 128, 768], P('dp'), may hold values from -56 to 56
- second: float32 [144, 128, 768], P('dp'), may hold values from 81.92 to 1310.72
- vec_master: float32 [12, 768], replicated
- vec_moment: float32 [12, 768], replicated, may hold values from -320 to 320
- vec_second: float32 [12, 768], replicated, may hold values from 3276.8 to 32768
Outputs:
- layer_out: bfloat16 [64, 512, 768], P('dp', 'seq')
- input_grad: float32 [64, 512, 768], P('dp', 'seq')
- residual_mid: float32 [64, 512, 768], P('dp', 'seq')
- sublayer_rms: float32 [64, 2], P('dp')
- grad_pool: float32 [144, 128, 768], P('dp')
- moment_new: float32 [144, 128, 768], P('dp')
- second_new: float32 [144, 128, 768], P('dp')
- master_new: float32 [144, 128, 768], P('dp')
- vec_grad: float32 [12, 768], replicated
- vec_moment_new: float32 [12, 768], replicated
- vec_second_new: float32 [12, 768], replicated
- vec_master_new: float32 [12, 768], replicated
Inputs may be any that keep to these rules, and one draw needn't show every extreme that they name: `lengths`: one sequence of each index of dp has length 512. Distinct slot numbers; block b lives in slot owner[b]. `master`: slots not named by owner hold values that only their own update reads.
All inputs are finite; a program needn't handle non-finite values.
Results may differ from a plain program's by a relative error of at most 0.025.
Values may be sent and summed in bfloat16 or wider, within the bound.
A program may use at most 320 MiB of HBM per device.

v0:
```python
from functools import partial

import jax
import jax.numpy as jnp
from jax import lax
from jax.sharding import PartitionSpec as P

D = 768
H = 12
DH = 64
FF = 3072
BLK = 128
STEP = 5


first_decay = 0.5
second_decay = 0.5
matrix_rate = 0.02
vector_rate = 0.2
weight_decay = 0.01
adam_epsilon = 1e-08


def passed_along(block, axis, distance):
    devices = range(lax.axis_size(axis))
    route = [((i - distance) % len(devices), i) for i in devices]
    return lax.ppermute(block, axis, route)


def norm_rows(resid, gain, shift):
    center = resid - jnp.mean(resid, axis=-1, keepdims=True)
    spread = jnp.mean(center * center, axis=-1, keepdims=True)
    return center * lax.rsqrt(spread + 1e-05) * gain + shift


def adam_step(gradient, moment, second, weight, rate):
    moment_new = first_decay * moment + (1.0 - first_decay) * gradient
    second_new = second_decay * second + (1.0 - second_decay) * gradient * gradient
    moment_hat = moment_new / (1.0 - first_decay**STEP)
    second_hat = second_new / (1.0 - second_decay**STEP)
    weight_new = weight - rate * (
        moment_hat / (jnp.sqrt(second_hat) + adam_epsilon) + weight_decay * weight
    )
    return (moment_new, second_new, weight_new)


def per_device(
    tokens, cotangent, lengths, owner, master, moment, second, vec_master, vec_moment, vec_second
):
    seq_count, block_len, width = tokens.shape
    seq_parts = lax.axis_size("seq")
    seq_place = lax.axis_index("seq")
    token_count = seq_count * block_len
    local_master = master.astype(jnp.bfloat16)
    gathered = lax.all_gather(local_master, "dp", axis=0, tiled=True)
    blocks = gathered[owner]
    square_count = D // BLK
    wide_count = FF // BLK
    w_query = blocks[0:square_count].reshape(D, D)
    w_key = blocks[square_count : 2 * square_count].reshape(D, D)
    w_value = blocks[2 * square_count : 3 * square_count].reshape(D, D)
    w_out = blocks[3 * square_count : 4 * square_count].reshape(D, D)
    w_up = blocks[4 * square_count : 4 * square_count + wide_count].reshape(FF, D)
    w_down = blocks[4 * square_count + wide_count :].reshape(FF, D)
    bias_up = vec_master[8:].reshape(FF)
    token_rows = tokens.reshape(token_count, D)
    rows_wide = token_rows.astype(jnp.float32)
    queries = (
        jnp.dot(token_rows, w_query, preferred_element_type=jnp.float32) + vec_master[0]
    ).astype(jnp.bfloat16)
    key_rows = jnp.dot(token_rows, w_key, preferred_element_type=jnp.float32).astype(jnp.bfloat16)
    value_rows = (
        jnp.dot(token_rows, w_value, preferred_element_type=jnp.float32) + vec_master[1]
    ).astype(jnp.bfloat16)
    shaped = (seq_count, block_len, H, DH)
    query_heads = queries.reshape(shaped)
    key_block = key_rows.reshape(shaped)
    value_block = value_rows.reshape(shaped)
    offsets = jnp.arange(block_len, dtype=jnp.int32)

    def key_mask(source):
        return ((source * block_len + offsets)[None, :] < lengths[:, None])[:, None, None, :]

    running = jnp.full((seq_count, H, block_len), -1e30, jnp.float32)
    totals = jnp.zeros((seq_count, H, block_len), jnp.float32)
    numerator = jnp.zeros(shaped, jnp.float32)
    kept_blocks = []
    for visit in range(seq_parts):
        if visit > 0:
            key_block, value_block = passed_along((key_block, value_block), "seq", 1)
        kept_blocks.append((key_block, value_block))
        valid_keys = key_mask((seq_place - visit) % seq_parts)
        scores = (
            jnp.einsum(
                "sqhe,skhe->shqk", query_heads, key_block, preferred_element_type=jnp.float32
            )
            * 0.125
        )
        masked = jnp.where(valid_keys, scores, -1e30)
        new_top = jnp.maximum(running, jnp.max(masked, axis=-1))
        expos = jnp.where(valid_keys, jnp.exp(masked - new_top[..., None]), 0.0)
        rescale = jnp.exp(running - new_top)
        totals = totals * rescale + jnp.sum(expos, axis=-1)
        update = jnp.einsum(
            "shqk,skhe->sqhe",
            expos.astype(jnp.bfloat16),
            value_block,
            preferred_element_type=jnp.float32,
        )
        numerator = numerator * jnp.transpose(rescale, (0, 2, 1))[..., None] + update
        running = new_top
    log_total = running + jnp.log(totals)
    context_wide = numerator / jnp.transpose(totals, (0, 2, 1))[..., None]
    context = context_wide.reshape(token_count, D).astype(jnp.bfloat16)
    branch = jnp.dot(context, w_out, preferred_element_type=jnp.float32) + vec_master[2]
    resid_first = rows_wide + branch
    middle = norm_rows(resid_first, vec_master[4], vec_master[5])
    middle_low = middle.astype(jnp.bfloat16)
    inner = jnp.einsum("td,fd->tf", middle_low, w_up, preferred_element_type=jnp.float32) + bias_up
    gelu_exact = partial(jax.nn.gelu, approximate=False)
    activ, gelu_back = jax.vjp(gelu_exact, inner)
    activ_low = activ.astype(jnp.bfloat16)
    feed = jnp.dot(activ_low, w_down, preferred_element_type=jnp.float32) + vec_master[3]
    resid_second = middle + feed
    result, second_back = jax.vjp(norm_rows, resid_second, vec_master[6], vec_master[7])
    layer_out = result.astype(jnp.bfloat16).reshape(seq_count, block_len, D)
    row_valid = ((seq_place * block_len + offsets)[None, :] < lengths[:, None]).astype(jnp.float32)
    row_mask = row_valid.reshape(token_count, 1)
    local_sums = jnp.stack(
        [
            jnp.sum((branch * branch * row_mask).reshape(seq_count, -1), axis=1),
            jnp.sum((feed * feed * row_mask).reshape(seq_count, -1), axis=1),
        ],
        axis=1,
    )
    summed = lax.psum(local_sums, "seq")
    sublayer_rms = jnp.sqrt(summed / (lengths[:, None].astype(jnp.float32) * D))
    upstream = cotangent.reshape(token_count, D).astype(jnp.float32) * row_mask
    d_second, grad_gain_second, grad_shift_second = second_back(upstream)
    d_feed = d_second.astype(jnp.bfloat16)
    grad_bias_down = jnp.sum(d_feed.astype(jnp.float32), axis=0)
    grad_w_down = jnp.einsum("tf,td->fd", activ_low, d_feed, preferred_element_type=jnp.float32)
    d_activ = jnp.einsum("td,fd->tf", d_feed, w_down, preferred_element_type=jnp.float32)
    d_inner = gelu_back(d_activ)[0].astype(jnp.bfloat16)
    grad_bias_up = jnp.sum(d_inner.astype(jnp.float32), axis=0)
    grad_w_up = jnp.einsum("tf,td->fd", d_inner, middle_low, preferred_element_type=jnp.float32)
    d_middle = jnp.dot(d_inner, w_up, preferred_element_type=jnp.float32) + d_second
    first_out, first_back = jax.vjp(norm_rows, resid_first, vec_master[4], vec_master[5])
    d_first, grad_gain_first, grad_shift_first = first_back(d_middle)
    d_branch = d_first.astype(jnp.bfloat16)
    grad_bias_out = jnp.sum(d_branch.astype(jnp.float32), axis=0)
    grad_w_out = jnp.einsum("td,te->de", context, d_branch, preferred_element_type=jnp.float32)
    d_context = jnp.einsum("te,de->td", d_branch, w_out, preferred_element_type=jnp.float32).astype(
        jnp.bfloat16
    )
    d_context_heads = d_context.reshape(shaped)
    delta = jnp.transpose(
        jnp.sum(d_context_heads.astype(jnp.float32) * context_wide, axis=-1), (0, 2, 1)
    )
    key_block = key_rows.reshape(shaped)
    value_block = value_rows.reshape(shaped)
    query_grad = jnp.zeros(shaped, jnp.float32)
    key_grad = jnp.zeros(shaped, jnp.float32)
    value_grad = jnp.zeros(shaped, jnp.float32)
    for visit in range(seq_parts):
        if visit > 0:
            key_block, value_block = passed_along((key_block, value_block), "seq", 1)
        valid_keys = key_mask((seq_place - visit) % seq_parts)
        scores = (
            jnp.einsum(
                "sqhe,skhe->shqk", query_heads, key_block, preferred_element_type=jnp.float32
            )
            * 0.125
        )
        masked = jnp.where(valid_keys, scores, -1e30)
        probs = jnp.where(valid_keys, jnp.exp(masked - log_total[..., None]), 0.0)
        value_grad = value_grad + jnp.einsum(
            "shqk,sqhe->skhe",
            probs.astype(jnp.bfloat16),
            d_context_heads,
            preferred_element_type=jnp.float32,
        )
        d_probs = jnp.einsum(
            "sqhe,skhe->shqk", d_context_heads, value_block, preferred_element_type=jnp.float32
        )
        d_scores = (probs * (d_probs - delta[..., None]) * 0.125).astype(jnp.bfloat16)
        query_grad = query_grad + jnp.einsum(
            "shqk,skhe->sqhe", d_scores, key_block, preferred_element_type=jnp.float32
        )
        key_grad = key_grad + jnp.einsum(
            "shqk,sqhe->skhe", d_scores, query_heads, preferred_element_type=jnp.float32
        )
        key_grad, value_grad = (
            passed_along(key_grad.astype(jnp.bfloat16), "seq", 1).astype(key_grad.dtype),
            passed_along(value_grad.astype(jnp.bfloat16), "seq", 1).astype(value_grad.dtype),
        )
    query_low = query_grad.reshape(token_count, D).astype(jnp.bfloat16)
    key_low = key_grad.reshape(token_count, D).astype(jnp.bfloat16)
    value_low = value_grad.reshape(token_count, D).astype(jnp.bfloat16)
    grad_bias_query = jnp.sum(query_low.astype(jnp.float32), axis=0)
    grad_bias_value = jnp.sum(value_low.astype(jnp.float32), axis=0)
    grad_w_query = jnp.einsum(
        "td,te->de", token_rows, query_low, preferred_element_type=jnp.float32
    )
    grad_w_key = jnp.einsum("td,te->de", token_rows, key_low, preferred_element_type=jnp.float32)
    grad_w_value = jnp.einsum(
        "td,te->de", token_rows, value_low, preferred_element_type=jnp.float32
    )
    input_grad = (
        d_first
        + jnp.einsum("te,de->td", query_low, w_query, preferred_element_type=jnp.float32)
        + jnp.einsum("te,de->td", key_low, w_key, preferred_element_type=jnp.float32)
        + jnp.einsum("te,de->td", value_low, w_value, preferred_element_type=jnp.float32)
    )
    vec_local = jnp.concatenate(
        [
            jnp.stack(
                [
                    grad_bias_query,
                    grad_bias_value,
                    grad_bias_out,
                    grad_bias_down,
                    grad_gain_first,
                    grad_shift_first,
                    grad_gain_second,
                    grad_shift_second,
                ],
                axis=0,
            ),
            grad_bias_up.reshape(FF // D, D),
        ],
        axis=0,
    )
    vec_grad = lax.psum(vec_local, ("dp", "seq"))
    flat_grad = jnp.concatenate(
        [
            matrix.reshape(-1, BLK, D)
            for matrix in (
                grad_w_query,
                grad_w_key,
                grad_w_value,
                grad_w_out,
                grad_w_up,
                grad_w_down,
            )
        ],
        axis=0,
    )
    slot_local = master.shape[0]
    dp_parts = lax.axis_size("dp")
    slot_total = slot_local * dp_parts
    slotted = jnp.zeros((slot_total, BLK, D), jnp.float32).at[owner].set(flat_grad)
    owned = lax.psum_scatter(slotted, "dp", scatter_dimension=0, tiled=True)
    grad_pool = lax.psum(owned.astype(jnp.bfloat16), "seq").astype(jnp.float32)
    moment_new, second_new, master_new = adam_step(grad_pool, moment, second, master, matrix_rate)
    vec_moment_new, vec_second_new, vec_master_new = adam_step(
        vec_grad, vec_moment, vec_second, vec_master, vector_rate
    )
    return (
        layer_out,
        input_grad.reshape(seq_count, block_len, D),
        middle.reshape(seq_count, block_len, D),
        sublayer_rms,
        grad_pool,
        moment_new,
        second_new,
        master_new,
        vec_grad,
        vec_moment_new,
        vec_second_new,
        vec_master_new,
    )


def solution(mesh):
    return jax.shard_map(
        per_device,
        mesh=mesh,
        in_specs=(
            P("dp", "seq", None),
            P("dp", "seq", None),
            P("dp"),
            P(),
            P("dp", None, None),
            P("dp", None, None),
            P("dp", None, None),
            P(),
            P(),
            P(),
        ),
        out_specs=(
            P("dp", "seq", None),
            P("dp", "seq", None),
            P("dp", "seq", None),
            P("dp", None),
            P("dp", None, None),
            P("dp", None, None),
            P("dp", None, None),
            P("dp", None, None),
            P(),
            P(),
            P(),
            P(),
        ),
        check_vma=False,
    )
```

profile of v0, /device:TPU:0, one launch (start us, length us, event | category | flops | bytes accessed | tf_op | source)
XLA Modules:
  0.0 1378.9 jit_solution(17909890057671230758)
XLA Ops:
  13.7 140.3 %all-gather.2.cloned.1.call-done = bf16[144,128,768]{2,1,0:T(8,128)(2,1)} async-done(((bf16[18,128,768]{2,1,0:T(8,128)(2,1)}), bf16[144,128,768]{2,1,0:T(8,128)(2,1)}) %all-gather.2.cloned.1.call-update) | async-done | bytes 28311568 | tf_op jit(solution)/shard_map/all_gather | solution.py:55
  154.0 16.8 %gather_fusion = bf16[72,128,768]{2,1,0:T(8,128)(2,1)} fusion(bf16[144,128,768]{2,1,0:T(8,128)(2,1)} %all-gather.2.cloned.1.call-done, s32[1024]{0:T(1024)S(1)} %pad_clamp_fusion), kind=kCustom, calls=%fused_computation | custom fusion | bytes 28311840 | tf_op jit(solution)/shard_map/gather | solution.py:56
  184.9 31.7 %collective-permute-done = bf16[8,128,12,64]{1,3,2,0:T(8,128)(2,1)} collective-permute-done((bf16[8,128,12,64]{1,3,2,0:T(8,128)(2,1)S(1)}, bf16[8,128,12,64]{1,3,2,0:T(8,128)(2,1)}, u32[]{:S(2)}, u32[]{:S(2)}) %collective-permute-start) | collective-permute-done | bytes 1572896 | tf_op jit(solution)/shard_map/ppermute | solution.py:27
  217.4 32.9 %collective-permute-done.1 = bf16[8,128,12,64]{1,3,2,0:T(8,128)(2,1)} collective-permute-done((bf16[8,128,12,64]{1,3,2,0:T(8,128)(2,1)}, bf16[8,128,12,64]{1,3,2,0:T(8,128)(2,1)}, u32[]{:S(2)}, u32[]{:S(2)}) %collective-permute-start.1) | collective-permute-done | bytes 1572896 | tf_op jit(solution)/shard_map/ppermute | solution.py:27
  254.2 29.9 %collective-permute-done.2 = bf16[8,128,12,64]{1,3,2,0:T(8,128)(2,1)} collective-permute-done((bf16[8,128,12,64]{1,3,2,0:T(8,128)(2,1)}, bf16[8,128,12,64]{1,3,2,0:T(8,128)(2,1)}, u32[]{:S(2)}, u32[]{:S(2)}) %collective-permute-start.2) | collective-permute-done | bytes 1572896 | tf_op jit(solution)/shard_map/ppermute | solution.py:27
  299.3 18.4 %collective-permute-done.3 = bf16[8,128,12,64]{1,3,2,0:T(8,128)(2,1)S(1)} collective-permute-done((bf16[8,128,12,64]{1,3,2,0:T(8,128)(2,1)}, bf16[8,128,12,64]{1,3,2,0:T(8,128)(2,1)S(1)}, u32[]{:S(2)}, u32[]{:S(2)}) %collective-permute-start.3) | collective-permute-done | bytes 1572896 | tf_op jit(solution)/shard_map/ppermute | solution.py:27
  321.4 30.0 %collective-permute-done.4 = bf16[8,128,12,64]{1,3,2,0:T(8,128)(2,1)S(1)} collective-permute-done((bf16[8,128,12,64]{1,3,2,0:T(8,128)(2,1)}, bf16[8,128,12,64]{1,3,2,0:T(8,128)(2,1)S(1)}, u32[]{:S(2)}, u32[]{:S(2)}) %collective-permute-start.4) | collective-permute-done | bytes 1572896 | tf_op jit(solution)/shard_map/ppermute | solution.py:27
  372.1 12.4 collective-permute-done.5
  396.6 34.3 %multiply_convert_fusion = (bf16[1024,3072]{1,0:T(8,128)(2,1)S(1)}, f32[1024,3072]{1,0:T(8,128)}, f32[1024,3072]{1,0:T(8,128)}) fusion(f32[3072]{0:T(1024)S(1)} %add.355, bf16[3072,768]{1,0:T(8,128)(2,1)S(1)} %bitcast.323, f32[1024,768]{1,0:T(8,128)S(1)} %multiply_add_fusion.1), kind=kOutput, calls=%fused_computation.6 | convolution fusion | flops 5040242688 | bytes 39333888 | tf_op jit(solution)/shard_map/td,fd->tf/dot_general | solution.py:119
  445.7 18.7 %convert_reduce_fusion = (f32[3072]{0:T(1024)}, bf16[1024,3072]{1,0:T(8,128)(2,1)}) fusion(f32[1024,3072]{1,0:T(8,128)} %get-tuple-element.45, bf16[1024,768]{1,0:T(8,128)(2,1)} %get-tuple-element.31, bf16[3072,768]{1,0:T(8,128)(2,1)} %bitcast.324, f32[1024,3072]{1,0:T(8,128)} %get-tuple-element.81, f32[3072]{0:T(1024)S(1)} %add.355), kind=kOutput, calls=%fused_computation.4 | convolution fusion | flops 4885312512 | bytes 37773312 | tf_op jit(solution)/shard_map/td,fd->tf/dot_general | solution.py:143
  540.7 27.7 %collective-permute-done.6 = bf16[8,128,12,64]{1,3,2,0:T(8,128)(2,1)S(1)} collective-permute-done((bf16[8,128,12,64]{1,3,2,0:T(8,128)(2,1)}, bf16[8,128,12,64]{1,3,2,0:T(8,128)(2,1)S(1)}, u32[]{:S(2)}, u32[]{:S(2)}) %collective-permute-start.6) | collective-permute-done | bytes 1572896 | tf_op jit(solution)/shard_map/ppermute | solution.py:27
  571.9 30.4 %collective-permute-done.10 = bf16[8,128,12,64]{1,3,2,0:T(8,128)(2,1)} collective-permute-done((bf16[8,128,12,64]{1,3,2,0:T(8,128)(2,1)}, bf16[8,128,12,64]{1,3,2,0:T(8,128)(2,1)}, u32[]{:S(2)}, u32[]{:S(2)}) %collective-permute-start.10) | collective-permute-done | bytes 1572896 | tf_op jit(solution)/shard_map/ppermute | solution.py:27
  615.8 20.1 %collective-permute-done.7 = bf16[8,128,12,64]{1,3,2,0:T(8,128)(2,1)S(1)} collective-permute-done((bf16[8,128,12,64]{1,3,2,0:T(8,128)(2,1)}, bf16[8,128,12,64]{1,3,2,0:T(8,128)(2,1)S(1)}, u32[]{:S(2)}, u32[]{:S(2)}) %collective-permute-start.7) | collective-permute-done | bytes 1572896 | tf_op jit(solution)/shard_map/ppermute | solution.py:27
  636.5 33.1 %collective-permute-done.11 = bf16[8,128,12,64]{1,3,2,0:T(8,128)(2,1)} collective-permute-done((bf16[8,128,12,64]{1,3,2,0:T(8,128)(2,1)}, bf16[8,128,12,64]{1,3,2,0:T(8,128)(2,1)}, u32[]{:S(2)}, u32[]{:S(2)}) %collective-permute-start.11) | collective-permute-done | bytes 1572896 | tf_op jit(solution)/shard_map/ppermute | solution.py:27
  678.1 25.1 %collective-permute-done.8 = bf16[8,128,12,64]{1,3,2,0:T(8,128)(2,1)S(1)} collective-permute-done((bf16[8,128,12,64]{1,3,2,0:T(8,128)(2,1)S(1)}, bf16[8,128,12,64]{1,3,2,0:T(8,128)(2,1)S(1)}, u32[]{:S(2)}, u32[]{:S(2)}) %collective-permute-start.8) | collective-permute-done | bytes 1572896 | tf_op jit(solution)/shard_map/ppermute | solution.py:27
  704.0 33.0 %collective-permute-done.12 = bf16[8,128,12,64]{1,3,2,0:T(8,128)(2,1)S(1)} collective-permute-done((bf16[8,128,12,64]{1,3,2,0:T(8,128)(2,1)S(1)}, bf16[8,128,12,64]{1,3,2,0:T(8,128)(2,1)S(1)}, u32[]{:S(2)}, u32[]{:S(2)}) %collective-permute-start.12) | collective-permute-done | bytes 1572896 | tf_op jit(solution)/shard_map/ppermute | solution.py:27
  745.2 25.4 %collective-permute-done.9 = bf16[8,128,12,64]{1,3,2,0:T(8,128)(2,1)S(1)} collective-permute-done((bf16[8,128,12,64]{1,3,2,0:T(8,128)(2,1)S(1)}, bf16[8,128,12,64]{1,3,2,0:T(8,128)(2,1)S(1)}, u32[]{:S(2)}, u32[]{:S(2)}) %collective-permute-start.9) | collective-permute-done | bytes 1572896 | tf_op jit(solution)/shard_map/ppermute | solution.py:27
  773.4 29.4 %collective-permute-done.13 = bf16[8,128,12,64]{1,3,2,0:T(8,128)(2,1)S(1)} collective-permute-done((bf16[8,128,12,64]{1,3,2,0:T(8,128)(2,1)S(1)}, bf16[8,128,12,64]{1,3,2,0:T(8,128)(2,1)S(1)}, u32[]{:S(2)}, u32[]{:S(2)}) %collective-permute-start.13) | collective-permute-done | bytes 1572896 | tf_op jit(solution)/shard_map/ppermute | solution.py:27
  822.4 18.0 %broadcast_in_dim.175 = f32[144,128,768]{2,1,0:T(8,128)} broadcast(f32[]{:T(128)} %constant.61.clone.1), dimensions={} | broadcast | bytes 56623108 | tf_op jit(solution)/shard_map/broadcast_in_dim | solution.py:252
  840.4 57.5 %scatter_fusion = f32[144,128,768]{2,1,0:T(8,128)} fusion(f32[144,128,768]{2,1,0:T(8,128)} %broadcast_in_dim.175, s32[72]{0:T(128)S(1)} %copy-done.69, f32[72,128,768]{2,1,0:T(8,128)} %constant_dynamic-update-slice_fusion), kind=kCustom, calls=%fused_computation.1 | custom fusion | bytes 84934944 | tf_op jit(solution)/shard_map/scatter | solution.py:252
  898.2 315.6 %reduce-scatter.2.cloned.1.call-done = f32[18,128,768]{2,1,0:T(8,128)} async-done(((f32[144,128,768]{2,1,0:T(8,128)}), f32[18,128,768]{2,1,0:T(8,128)}) %reduce-scatter.2.cloned.1.call-update) | async-done | bytes 7077904 | tf_op jit(solution)/shard_map/reduce_scatter | solution.py:253
  1237.8 43.1 %psum.23 = f32[12,768]{1,0:T(8,128)S(1)} all-reduce(f32[12,768]{1,0:T(8,128)S(1)} %concatenate.7), channel_id=1, replica_groups=mesh['dp'=8,'seq'=4] {'dp','seq'}, use_global_device_ids=true, to_apply=%region_34.35 | all-reduce | flops 9216 | bytes 73728 | tf_op jit(solution)/shard_map/psum | solution.py:234
  1289.0 65.1 %all-reduce.2.cloned.1.call-done = bf16[18,128,768]{2,1,0:T(8,128)(2,1)} async-done(((bf16[18,128,768]{2,1,0:T(8,128)(2,1)}), bf16[18,128,768]{2,1,0:T(8,128)(2,1)}) %all-reduce.2.cloned.1.call-update) | async-done | bytes 3538960 | tf_op jit(solution)/shard_map/psum | solution.py:254
  1354.1 17.8 %multiply_subtract_fusion = (f32[18,128,768]{2,1,0:T(8,128)}, f32[18,128,768]{2,1,0:T(8,128)}, f32[18,128,768]{2,1,0:T(8,128)}, f32[18,128,768]{2,1,0:T(8,128)}) fusion(f32[18,128,768]{2,1,0:T(8,128)} %param.14, f32[18,128,768]{2,1,0:T(8,128)} %param.16, f32[18,128,768]{2,1,0:T(8,128)} %param.15, bf16[18,128,768]{2,1,0:T(8,128)(2,1)} %all-reduce.2.cloned.1.call-done), kind=kLoop, calls=%fused_computation.23 | loop fusion | flops 26542080 | bytes 53084160 | tf_op jit(solution)/shard_map/sub | solution.py:41
  (342 shorter events, 256.6 us)
Async XLA Ops:
  7.2 146.8 %all-gather.2.cloned.1.call-start = ((), (), s32[]{:S(2)}) async-start(), calls=%async_computation.1 | async-start | bytes 31850496 | tf_op jit(solution)/shard_map/all_gather | solution.py:55
  12.5 1201.2 %reduce-scatter.2.cloned.1.call-start = ((), (), s32[]{:S(2)}) async-start(), calls=%async_computation.2 | async-start | bytes 63700992 | tf_op jit(solution)/shard_map/reduce_scatter | solution.py:253
  177.1 107.0 %copy-start.7 = (bf16[96,8,8,128]{3,2,1,0:T(8,128)(2,1)}, bf16[96,8,8,128]{3,2,1,0:T(8,128)(2,1)S(1)}, u32[]{:S(2)}) copy-start(bf16[96,8,8,128]{3,2,1,0:T(8,128)(2,1)S(1)} %copy.221) | copy-start | bytes 4718596
  177.5 39.2 %collective-permute-start = (bf16[8,128,12,64]{1,3,2,0:T(8,128)(2,1)S(1)}, bf16[8,128,12,64]{1,3,2,0:T(8,128)(2,1)}, u32[]{:S(2)}, u32[]{:S(2)}) collective-permute-start(bf16[8,128,12,64]{1,3,2,0:T(8,128)(2,1)S(1)} %copy.153), channel_id=1, source_target_pairs={{3,0},{0,1},{1,2},{2,3},{7,4},{4,5},{5,6},{6,7},{11,8},{8,9},{9,10... | collective-permute-start | bytes 4718600 | tf_op jit(solution)/shard_map/ppermute | solution.py:27
  181.8 187.4 %copy-start.16 = (bf16[96,8,8,128]{3,2,1,0:T(8,128)(2,1)}, bf16[96,8,8,128]{3,2,1,0:T(8,128)(2,1)S(1)}, u32[]{:S(2)}) copy-start(bf16[96,8,8,128]{3,2,1,0:T(8,128)(2,1)S(1)} %copy.222) | copy-start | bytes 4718596
  183.4 66.9 %collective-permute-start.1 = (bf16[8,128,12,64]{1,3,2,0:T(8,128)(2,1)}, bf16[8,128,12,64]{1,3,2,0:T(8,128)(2,1)}, u32[]{:S(2)}, u32[]{:S(2)}) collective-permute-start(bf16[8,128,12,64]{1,3,2,0:T(8,128)(2,1)} %copy.154), channel_id=1, source_target_pairs={{3,0},{0,1},{1,2},{2,3},{7,4},{4,5},{5,6},{6,7},{11,8},{8,9},{9,10... | collective-permute-start | bytes 4718600 | tf_op jit(solution)/shard_map/ppermute | solution.py:27
  216.7 67.4 %collective-permute-start.2 = (bf16[8,128,12,64]{1,3,2,0:T(8,128)(2,1)}, bf16[8,128,12,64]{1,3,2,0:T(8,128)(2,1)}, u32[]{:S(2)}, u32[]{:S(2)}) collective-permute-start(bf16[8,128,12,64]{1,3,2,0:T(8,128)(2,1)} %collective-permute-done), channel_id=1, source_target_pairs={{3,0},{0,1},{1,2},{2,3},{7,4},{4,5},{5,6},{6,7},{11,8},{8,9},{9,10... | collective-permute-start | bytes 4718600 | tf_op jit(solution)/shard_map/ppermute | solution.py:27
  217.4 144.4 %copy-start.62 = (pred[8,128]{1,0:T(8,128)(4,1)}, pred[8,128]{1,0:T(8,128)(4,1)S(1)}, u32[]{:S(2)}) copy-start(pred[8,128]{1,0:T(8,128)(4,1)S(1)} %get-tuple-element.66) | copy-start | bytes 3076
  217.4 148.4 %copy-start.60 = (pred[8,128]{1,0:T(8,128)(4,1)}, pred[8,128]{1,0:T(8,128)(4,1)S(1)}, u32[]{:S(2)}) copy-start(pred[8,128]{1,0:T(8,128)(4,1)S(1)} %get-tuple-element.67) | copy-start | bytes 3076
  217.4 151.7 %copy-start.66 = (pred[8,128]{1,0:T(8,128)(4,1)}, pred[8,128]{1,0:T(8,128)(4,1)S(1)}, u32[]{:S(2)}) copy-start(pred[8,128]{1,0:T(8,128)(4,1)S(1)} %get-tuple-element.69) | copy-start | bytes 3076
  217.4 167.0 %copy-start.58 = (pred[8,128]{1,0:T(8,128)(4,1)}, pred[8,128]{1,0:T(8,128)(4,1)S(1)}, u32[]{:S(2)}) copy-start(pred[8,128]{1,0:T(8,128)(4,1)S(1)} %get-tuple-element.68) | copy-start | bytes 3076
  250.4 67.3 %collective-permute-start.3 = (bf16[8,128,12,64]{1,3,2,0:T(8,128)(2,1)}, bf16[8,128,12,64]{1,3,2,0:T(8,128)(2,1)S(1)}, u32[]{:S(2)}, u32[]{:S(2)}) collective-permute-start(bf16[8,128,12,64]{1,3,2,0:T(8,128)(2,1)} %collective-permute-done.1), channel_id=1, source_target_pairs={{3,0},{0,1},{1,2},{2,3},{7,4},{4,5},{5,6},{6,7},{11,8},{8,9},{9,10... | collective-permute-start | bytes 4718600 | tf_op jit(solution)/shard_map/ppermute | solution.py:27
  254.2 97.2 %copy-start = (bf16[96,8,8,128]{3,2,1,0:T(8,128)(2,1)}, bf16[96,8,8,128]{3,2,1,0:T(8,128)(2,1)S(1)}, u32[]{:S(2)}) copy-start(bf16[96,8,8,128]{3,2,1,0:T(8,128)(2,1)S(1)} %copy.220) | copy-start | bytes 4718596
  284.1 67.3 %collective-permute-start.4 = (bf16[8,128,12,64]{1,3,2,0:T(8,128)(2,1)}, bf16[8,128,12,64]{1,3,2,0:T(8,128)(2,1)S(1)}, u32[]{:S(2)}, u32[]{:S(2)}) collective-permute-start(bf16[8,128,12,64]{1,3,2,0:T(8,128)(2,1)} %collective-permute-done.2), channel_id=1, source_target_pairs={{3,0},{0,1},{1,2},{2,3},{7,4},{4,5},{5,6},{6,7},{11,8},{8,9},{9,10... | collective-permute-start | bytes 4718600 | tf_op jit(solution)/shard_map/ppermute | solution.py:27
  317.7 66.7 %collective-permute-start.5 = (bf16[8,128,12,64]{1,3,2,0:T(8,128)(2,1)S(1)}, bf16[8,128,12,64]{1,3,2,0:T(8,128)(2,1)S(1)}, u32[]{:S(2)}, u32[]{:S(2)}) collective-permute-start(bf16[8,128,12,64]{1,3,2,0:T(8,128)(2,1)S(1)} %collective-permute-done.3), channel_id=1, source_target_pairs={{3,0},{0,1},{1,2},{2,3},{7,4},{4,5},{5,6},{6,7},{11,8},{8,9},{9,10... | collective-permute-start | bytes 4718600 | tf_op jit(solution)/shard_map/ppermute | solution.py:27
  529.0 39.4 %collective-permute-start.6 = (bf16[8,128,12,64]{1,3,2,0:T(8,128)(2,1)}, bf16[8,128,12,64]{1,3,2,0:T(8,128)(2,1)S(1)}, u32[]{:S(2)}, u32[]{:S(2)}) collective-permute-start(bf16[8,128,12,64]{1,3,2,0:T(8,128)(2,1)} %fusion.108), channel_id=1, source_target_pairs={{3,0},{0,1},{1,2},{2,3},{7,4},{4,5},{5,6},{6,7},{11,8},{8,9},{9,10... | collective-permute-start | bytes 4718600 | tf_op jit(solution)/shard_map/ppermute | solution.py:27
  529.1 73.1 %collective-permute-start.10 = (bf16[8,128,12,64]{1,3,2,0:T(8,128)(2,1)}, bf16[8,128,12,64]{1,3,2,0:T(8,128)(2,1)}, u32[]{:S(2)}, u32[]{:S(2)}) collective-permute-start(bf16[8,128,12,64]{1,3,2,0:T(8,128)(2,1)} %fusion.110), channel_id=1, source_target_pairs={{3,0},{0,1},{1,2},{2,3},{7,4},{4,5},{5,6},{6,7},{11,8},{8,9},{9,10... | collective-permute-start | bytes 4718600 | tf_op jit(solution)/shard_map/ppermute | solution.py:27
  571.9 64.0 %collective-permute-start.7 = (bf16[8,128,12,64]{1,3,2,0:T(8,128)(2,1)}, bf16[8,128,12,64]{1,3,2,0:T(8,128)(2,1)S(1)}, u32[]{:S(2)}, u32[]{:S(2)}) collective-permute-start(bf16[8,128,12,64]{1,3,2,0:T(8,128)(2,1)} %fusion.44), channel_id=1, source_target_pairs={{3,0},{0,1},{1,2},{2,3},{7,4},{4,5},{5,6},{6,7},{11,8},{8,9},{9,10... | collective-permute-start | bytes 4718600 | tf_op jit(solution)/shard_map/ppermute | solution.py:27
  607.0 62.7 %collective-permute-start.11 = (bf16[8,128,12,64]{1,3,2,0:T(8,128)(2,1)}, bf16[8,128,12,64]{1,3,2,0:T(8,128)(2,1)}, u32[]{:S(2)}, u32[]{:S(2)}) collective-permute-start(bf16[8,128,12,64]{1,3,2,0:T(8,128)(2,1)} %fusion.41), channel_id=1, source_target_pairs={{3,0},{0,1},{1,2},{2,3},{7,4},{4,5},{5,6},{6,7},{11,8},{8,9},{9,10... | collective-permute-start | bytes 4718600 | tf_op jit(solution)/shard_map/ppermute | solution.py:27
  636.5 66.8 %collective-permute-start.8 = (bf16[8,128,12,64]{1,3,2,0:T(8,128)(2,1)S(1)}, bf16[8,128,12,64]{1,3,2,0:T(8,128)(2,1)S(1)}, u32[]{:S(2)}, u32[]{:S(2)}) collective-permute-start(bf16[8,128,12,64]{1,3,2,0:T(8,128)(2,1)S(1)} %fusion.43), channel_id=1, source_target_pairs={{3,0},{0,1},{1,2},{2,3},{7,4},{4,5},{5,6},{6,7},{11,8},{8,9},{9,10... | collective-permute-start | bytes 4718600 | tf_op jit(solution)/shard_map/ppermute | solution.py:27
  671.6 65.3 %collective-permute-start.12 = (bf16[8,128,12,64]{1,3,2,0:T(8,128)(2,1)S(1)}, bf16[8,128,12,64]{1,3,2,0:T(8,128)(2,1)S(1)}, u32[]{:S(2)}, u32[]{:S(2)}) collective-permute-start(bf16[8,128,12,64]{1,3,2,0:T(8,128)(2,1)S(1)} %fusion.40), channel_id=1, source_target_pairs={{3,0},{0,1},{1,2},{2,3},{7,4},{4,5},{5,6},{6,7},{11,8},{8,9},{9,10... | collective-permute-start | bytes 4718600 | tf_op jit(solution)/shard_map/ppermute | solution.py:27
  703.9 66.8 %collective-permute-start.9 = (bf16[8,128,12,64]{1,3,2,0:T(8,128)(2,1)S(1)}, bf16[8,128,12,64]{1,3,2,0:T(8,128)(2,1)S(1)}, u32[]{:S(2)}, u32[]{:S(2)}) collective-permute-start(bf16[8,128,12,64]{1,3,2,0:T(8,128)(2,1)S(1)} %fusion.42), channel_id=1, source_target_pairs={{3,0},{0,1},{1,2},{2,3},{7,4},{4,5},{5,6},{6,7},{11,8},{8,9},{9,10... | collective-permute-start | bytes 4718600 | tf_op jit(solution)/shard_map/ppermute | solution.py:27
  737.6 65.2 %collective-permute-start.13 = (bf16[8,128,12,64]{1,3,2,0:T(8,128)(2,1)S(1)}, bf16[8,128,12,64]{1,3,2,0:T(8,128)(2,1)S(1)}, u32[]{:S(2)}, u32[]{:S(2)}) collective-permute-start(bf16[8,128,12,64]{1,3,2,0:T(8,128)(2,1)S(1)} %fusion.39), channel_id=1, source_target_pairs={{3,0},{0,1},{1,2},{2,3},{7,4},{4,5},{5,6},{6,7},{11,8},{8,9},{9,10... | collective-permute-start | bytes 4718600 | tf_op jit(solution)/shard_map/ppermute | solution.py:27
  897.9 456.2 %all-reduce.2.cloned.1.call-start = ((), (), s32[]{:S(2)}) async-start(), calls=%async_computation.3 | async-start | bytes 7077888 | tf_op jit(solution)/shard_map/psum | solution.py:254
  (92 other events, 1090.4 us)
Sparse Core Ops, SparseCore 0:
  12.6 141.3 all-gather.1
  898.0 315.6 reduce-scatter.1
  1219.3 134.7 all-reduce.1
where the time goes:
time: 1390 us; the launch traced here: 1380 us
  waiting for transfers between devices  900 us (65%)
  matrix products  199 us (14%)
  local copies, waits for them, and re-layouts  147 us (11%)
  other arithmetic  56.9 us (4%)
  blocking collectives  55.1 us (4%)
  between operations  15.6 us (1%)
    ppermute x14, waiting for transfers between devices, passed_along(): return lax.ppermute(block, axis, route)  379 us
    reduce_scatter x1, waiting for transfers between devices, per_device(): owned = lax.psum_scatter(slotted, 'dp', scatter_dimension=0, tiled=True)  316 us
    all_gather x1, waiting for transfers between devices, per_device(): gathered = lax.all_gather(local_master, 'dp', axis=0, tiled=True)  140 us
    psum x1, waiting for transfers between devices, per_device(): grad_pool = lax.psum(owned.astype(jnp.bfloat16), 'seq').astype(jnp.float32)  65.1 us
    scatter x1, local copies, waits for them, and re-layouts, per_device(): jnp.zeros((slot_total, BLK, D), jnp.float32).at[owner].set(flat_grad)  57.5 us
    psum x1, blocking collectives, per_device(): vec_grad = lax.psum(vec_local, ('dp', 'seq'))  43.1 us
    dot_general x1, matrix products, per_device(): jnp.einsum('td,fd->tf', middle_low, w_up, preferred_element_type=jnp.floa...  34.3 us
  transfers between devices with their start and end apart: 17, of which 17 were waited for; matrix products, arithmetic and copies ran while one was open for 8% of the time, Pallas kernels for 0%

commit v1 on v0

v1 whole, which is shorter than its diff:
```python
from functools import partial

import jax
import jax.numpy as jnp
from jax import lax
from jax.experimental import pallas as pl
from jax.experimental.pallas import tpu as pltpu
from jax.sharding import PartitionSpec as P

D = 768
H = 12
DH = 64
FF = 3072
BLK = 128
SEQLEN = 512
STEP = 5


first_decay = 0.5
second_decay = 0.5
matrix_rate = 0.02
vector_rate = 0.2
weight_decay = 0.01
adam_epsilon = 1e-08


def adam_step(gradient, moment, second, weight, rate):
    moment_new = first_decay * moment + (1.0 - first_decay) * gradient
    second_new = second_decay * second + (1.0 - second_decay) * gradient * gradient
    moment_hat = moment_new * (1.0 / (1.0 - first_decay**STEP))
    second_hat = second_new * (1.0 / (1.0 - second_decay**STEP))
    root = second_hat * lax.rsqrt(second_hat) + adam_epsilon
    inverse = pltpu.reciprocal(root, approx=True)
    inverse = inverse * (2.0 - root * inverse)
    weight_new = weight - rate * (moment_hat * inverse + weight_decay * weight)
    return (moment_new, second_new, weight_new)


def seq_swap(parts, axis):
    size = lax.axis_size(axis)
    me = lax.axis_index(axis)
    stacked = parts
    got = [None] * size
    mine = lax.dynamic_index_in_dim(stacked, me, 0, keepdims=False)
    out = [mine]
    for hop in range(1, size):
        there = jnp.bitwise_xor(me, hop)
        piece = lax.dynamic_index_in_dim(stacked, there, 0, keepdims=False)
        route = [(i, i ^ hop) for i in range(size)]
        out.append(lax.ppermute(piece, axis, route))
    return out


def from_hops(pieces, axis):
    size = lax.axis_size(axis)
    me = lax.axis_index(axis)
    stacked = jnp.stack(pieces, axis=0)
    order = jnp.bitwise_xor(jnp.arange(size, dtype=jnp.int32), me)
    return jnp.take(stacked, order, axis=0)


def to_whole(block, axis):
    size = lax.axis_size(axis)
    count, length, width = block.shape
    pieces = seq_swap(block.reshape(size, count // size, length, width), axis)
    stacked = from_hops(pieces, axis)
    return jnp.swapaxes(stacked, 0, 1).reshape(count // size, size * length, width)


def to_split(whole, axis):
    size = lax.axis_size(axis)
    own, full, width = whole.shape
    parts = jnp.swapaxes(whole.reshape(own, size, full // size, width), 0, 1)
    pieces = seq_swap(parts, axis)
    return from_hops(pieces, axis).reshape(size * own, full // size, width)


LANES = 128
PAIRS = D // LANES
CHUNKS = FF // D
MASKED = -1e30
NT = (((1,), (1,)), ((), ()))
TN = (((0,), (0,)), ((), ()))
MIB = 1 << 20


def mm(left, right):
    return jnp.dot(left, right, preferred_element_type=jnp.float32)


def mm_nt(left, right):
    return lax.dot_general(left, right, NT, preferred_element_type=jnp.float32)


def mm_tn(left, right):
    return lax.dot_general(left, right, TN, preferred_element_type=jnp.float32)


def load_blocks(pool_ref, place_ref, first, into_ref, sem):
    def start(i, _):
        pltpu.make_async_copy(
            pool_ref.at[place_ref[first + i]], into_ref.at[pl.ds(i * BLK, BLK)], sem
        ).start()
        return 0

    lax.fori_loop(0, into_ref.shape[0] // BLK, start, 0)


def wait_whole(ref, sem):
    pltpu.make_async_copy(ref, ref, sem).wait()


def spare_lanes(rows, half, bias_column):
    lane = lax.broadcasted_iota(jnp.int32, (rows, LANES), 1)
    first = DH * (1 - half)
    spare = jnp.where(lane == first, bias_column, jnp.where(lane < first + 4, 1.0, 0.0))
    inside = (lane >= DH * half) & (lane < DH * half + DH)
    return inside, spare.astype(jnp.bfloat16)


def split3(row):
    one = row.astype(jnp.bfloat16)
    rest = row - one.astype(jnp.float32)
    two = rest.astype(jnp.bfloat16)
    three = (rest - two.astype(jnp.float32)).astype(jnp.bfloat16)
    return one, two, three


def beside(head_rows, extra, half):
    columns = head_rows.shape[1]
    pad = jnp.zeros((DH - extra.shape[0], columns), jnp.bfloat16)
    parts = [extra.astype(jnp.bfloat16), pad]
    order = [head_rows] + parts if half == 0 else parts + [head_rows]
    return jnp.concatenate(order, axis=0)


def forward_pair(q_ref, k_ref, v_ref, ctx_ref, lse_ref, seq, p, bias):
    rows = q_ref.shape[0]
    cols = pl.ds(pl.multiple_of(p * LANES, LANES), LANES)
    row8 = lax.broadcasted_iota(jnp.int32, (16, rows), 0)
    q2t = q_ref[:, cols].T
    k2 = k_ref[:, cols]
    v2t = v_ref[:, cols].T
    outs = []
    for half in range(2):
        inside, spare = spare_lanes(rows, half, bias)
        k_aug = jnp.where(inside, k2, spare)
        head = slice(half * DH, half * DH + DH)
        q_aug = beside(q2t[head], jnp.where(row8 == 0, 1.0, 0.0), half)
        scores = mm(k_aug, q_aug)
        top = jnp.max(scores, axis=0, keepdims=True)
        expos = jnp.exp(scores - top).astype(jnp.bfloat16)
        v_aug = jnp.concatenate([v2t[head], jnp.ones((16, rows), jnp.bfloat16)], axis=0)
        both = mm(v_aug, expos)
        total = both[DH : DH + 1]
        outs.append(both[0:DH] / total)
        lse_ref[seq, pl.ds(2 * p + half, 1), :] = top + jnp.log(total)
    ctx_ref[:, cols] = jnp.concatenate(outs, axis=0).T.astype(jnp.bfloat16)


def attend_kernel(
    place_ref, lengths_ref, tokens_ref, pool_ref, vec_ref,
    q_ref, k_ref, v_ref, ctx_ref, lse_ref, w_scr,
    sem,
):
    seq = pl.program_id(0)
    rows = tokens_ref.shape[0]

    @pl.when(seq == 0)
    def _():
        load_blocks(pool_ref, place_ref, 0, w_scr, sem)
        wait_whole(w_scr, sem)

    tokens = tokens_ref[...]
    q_ref[...] = ((mm(tokens, w_scr[0:D, :]) + vec_ref[0:1, :]).astype(jnp.bfloat16) * 0.125).astype(jnp.bfloat16)
    k_ref[...] = mm(tokens, w_scr[D : 2 * D, :]).astype(jnp.bfloat16)
    v_ref[...] = (mm(tokens, w_scr[2 * D :, :]) + vec_ref[1:2, :]).astype(jnp.bfloat16)
    key = lax.broadcasted_iota(jnp.int32, (rows, 1), 0)
    bias = jnp.where(key < lengths_ref[seq], 0.0, MASKED)

    def pair(p, _):
        forward_pair(q_ref, k_ref, v_ref, ctx_ref, lse_ref, 0, p, bias)
        return 0

    lax.fori_loop(0, PAIRS, pair, 0)


def attend(place, lengths, tokens, pool, vec):
    seqs, rows, _ = tokens.shape
    flat = tokens.reshape(seqs * rows, D)
    row_spec = pl.BlockSpec((rows, D), lambda s, *_: (s, 0))
    any_spec = pl.BlockSpec(memory_space=pl.ANY)
    low = jax.ShapeDtypeStruct((seqs * rows, D), jnp.bfloat16)
    return pl.pallas_call(
        attend_kernel,
        grid_spec=pltpu.PrefetchScalarGridSpec(
            num_scalar_prefetch=2,
            grid=(seqs,),
            in_specs=[row_spec, any_spec, pl.BlockSpec(vec.shape, lambda s, *_: (0, 0))],
            out_specs=[row_spec] * 4
            + [
                pl.BlockSpec((1, 16, rows), lambda s, *_: (s, 0, 0)),
                pl.BlockSpec((3 * D, D), lambda s, *_: (0, 0)),
            ],
            scratch_shapes=[pltpu.SemaphoreType.DMA],
        ),
        out_shape=[low] * 4
        + [
            jax.ShapeDtypeStruct((seqs, 16, rows), jnp.float32),
            jax.ShapeDtypeStruct((3 * D, D), jnp.bfloat16),
        ],
        compiler_params=pltpu.CompilerParams(vmem_limit_bytes=48 * MIB),
        cost_estimate=pl.CostEstimate(
            flops=6 * seqs * rows * D * D + 4 * seqs * rows * rows * D,
            bytes_accessed=10 * seqs * rows * D + 6 * D * D,
            transcendentals=seqs * rows * rows * H,
        ),
        name="attend",
    )(place, lengths, flat, pool, vec)


def gelu_parts(x):
    z = jnp.abs(x) * 0.7071067811865476
    t_in = 1.0 + 0.3275911 * z
    t = pltpu.reciprocal(t_in, approx=True)
    t = t * (2.0 - t_in * t)
    e = jnp.exp(-0.5 * (x * x))
    poly = 1.061405429 * t - 1.453152027
    poly = poly * t + 1.421413741
    poly = poly * t - 0.284496736
    poly = poly * t + 0.254829592
    tail = (0.5 * t) * poly * e
    dist = jnp.where(x >= 0, 1.0 - tail, tail)
    return dist, x * e * 0.3989422804014327


def norm_stats(resid):
    center = resid - jnp.mean(resid, axis=-1, keepdims=True)
    scale = lax.rsqrt(jnp.mean(center * center, axis=-1, keepdims=True) + 1e-05)
    return center * scale, scale


def norm_back(d_out, gain, hat, scale):
    d_hat = d_out * gain
    mean_one = jnp.mean(d_hat, axis=-1, keepdims=True)
    mean_hat = jnp.mean(d_hat * hat, axis=-1, keepdims=True)
    return scale * (d_hat - mean_one - hat * mean_hat)


def feed_kernel(
    place_ref, lengths_ref, tokens_ref, ctx_ref, cot_ref, pool_ref, vec_ref,
    wide_mid_ref, mid_ref, out_ref, act_ref, dinner_ref, dfeed_ref, dbranch_ref, dres_ref, dctx_ref, grad_ref, sq_ref,
    w_out, w_up, w_down, slope_scr, sem, *, seq_rows,
):
    step = pl.program_id(0)
    rows = tokens_ref.shape[0]
    tiles = sq_ref.shape[0]
    first = 3 * D // BLK

    @pl.when(step == 0)
    def _():
        load_blocks(pool_ref, place_ref, first, w_out, sem.at[0])
        load_blocks(pool_ref, place_ref, first + D // BLK, w_up, sem.at[1])
        load_blocks(pool_ref, place_ref, first + (D + FF) // BLK, w_down, sem.at[2])
        wait_whole(w_out, sem.at[0])
        grad_ref[...] = jnp.zeros_like(grad_ref)

    def add_row(row, value):
        grad_ref[row : row + 1, :] += jnp.sum(value, axis=0, keepdims=True)

    segment = min(rows, seq_rows)
    row = lax.broadcasted_iota(jnp.int32, (rows, 1), 0)
    length = jnp.zeros((rows, 1), jnp.int32)
    for j in range(rows // segment):
        length = jnp.where(row // segment == j, lengths_ref[(step * rows + j * segment) // seq_rows], length)
    place_in = (step * rows + row) % seq_rows
    if seq_rows < SEQLEN:
        place_in += lax.axis_index("seq") * seq_rows
    valid = (place_in < length).astype(jnp.float32)

    def square_sums(which, value):
        square = value * value * valid
        for j in range(rows // segment):
            sq_ref[0, 2 * j + which : 2 * j + which + 1, :] = jnp.sum(
                square[j * segment : (j + 1) * segment], axis=0, keepdims=True
            )

    branch = mm(ctx_ref[...], w_out[...]) + vec_ref[2:3, :]
    square_sums(0, branch)
    hat1, scale1 = norm_stats(tokens_ref[...].astype(jnp.float32) + branch)
    middle = hat1 * vec_ref[4:5, :] + vec_ref[5:6, :]
    wide_mid_ref[...] = middle
    mid_ref[...] = middle.astype(jnp.bfloat16)
    mid_low = mid_ref[...]

    @pl.when(step == 0)
    def _():
        wait_whole(w_up, sem.at[1])
        wait_whole(w_down, sem.at[2])

    feed = jnp.zeros((rows, D), jnp.float32) + vec_ref[3:4, :]
    for c in range(CHUNKS):
        part = slice(c * D, (c + 1) * D)
        inner = mm_nt(mid_low, w_up[part, :]) + vec_ref[8 + c : 9 + c, :]
        dist, bell = gelu_parts(inner)
        act = (inner * dist).astype(jnp.bfloat16)
        act_ref[:, part] = act
        slope_scr[:, part] = dist + bell
        feed += mm(act, w_down[part, :])
    square_sums(1, feed)
    hat2, scale2 = norm_stats(middle + feed)
    gain2 = vec_ref[6:7, :]
    out_ref[...] = (hat2 * gain2 + vec_ref[7:8, :]).astype(jnp.bfloat16)
    upstream = cot_ref[...].astype(jnp.float32) * valid
    add_row(6, upstream * hat2)
    add_row(7, upstream)
    d_res2 = norm_back(upstream, gain2, hat2, scale2)
    d_feed = d_res2.astype(jnp.bfloat16)
    dfeed_ref[...] = d_feed
    add_row(3, d_feed.astype(jnp.float32))
    d_mid = d_res2
    for c in range(CHUNKS):
        part = slice(c * D, (c + 1) * D)
        d_inner = (mm_nt(d_feed, w_down[part, :]) * slope_scr[:, part]).astype(jnp.bfloat16)
        dinner_ref[:, part] = d_inner
        add_row(8 + c, d_inner.astype(jnp.float32))
        d_mid += mm(d_inner, w_up[part, :])
    add_row(4, d_mid * hat1)
    add_row(5, d_mid)
    d_res1 = norm_back(d_mid, vec_ref[4:5, :], hat1, scale1)
    dres_ref[...] = d_res1
    d_branch = d_res1.astype(jnp.bfloat16)
    dbranch_ref[...] = d_branch
    add_row(2, d_branch.astype(jnp.float32))
    dctx_ref[...] = mm_nt(d_branch, w_out[...]).astype(jnp.bfloat16)


def feed_both(place, lengths, seq_rows, tokens, ctx, cot, pool, vec, tile=256):
    total = tokens.shape[0]
    steps = total // tile
    row_spec = pl.BlockSpec((tile, D), lambda s, *_: (s, 0))
    wide_spec = pl.BlockSpec((tile, FF), lambda s, *_: (s, 0))
    any_spec = pl.BlockSpec(memory_space=pl.ANY)
    low = jax.ShapeDtypeStruct((total, D), jnp.bfloat16)
    wide = jax.ShapeDtypeStruct((total, FF), jnp.bfloat16)
    return pl.pallas_call(
        partial(feed_kernel, seq_rows=seq_rows),
        grid_spec=pltpu.PrefetchScalarGridSpec(
            num_scalar_prefetch=2,
            grid=(steps,),
            in_specs=[row_spec] * 3 + [any_spec, pl.BlockSpec(vec.shape, lambda s, *_: (0, 0))],
            out_specs=[row_spec, row_spec, row_spec, wide_spec, wide_spec, row_spec, row_spec, row_spec, row_spec,
                pl.BlockSpec((16, D), lambda s, *_: (0, 0)),
                pl.BlockSpec((1, 8, D), lambda s, *_: (s, 0, 0))],
            scratch_shapes=[
                pltpu.VMEM((D, D), jnp.bfloat16),
                pltpu.VMEM((FF, D), jnp.bfloat16),
                pltpu.VMEM((FF, D), jnp.bfloat16),
                pltpu.VMEM((tile, FF), jnp.float32),
                pltpu.SemaphoreType.DMA((3,)),
            ],
        ),
        out_shape=[jax.ShapeDtypeStruct((total, D), jnp.float32), low, low, wide, wide, low, low, jax.ShapeDtypeStruct((total, D), jnp.float32), low,
            jax.ShapeDtypeStruct((16, D), jnp.float32),
            jax.ShapeDtypeStruct((steps, 8, D), jnp.float32)],
        compiler_params=pltpu.CompilerParams(vmem_limit_bytes=56 * MIB),
        cost_estimate=pl.CostEstimate(
            flops=8 * total * D * FF + 4 * total * D * D,
            bytes_accessed=total * (16 * D + 4 * FF) + 12 * FF * D,
            transcendentals=total * FF,
        ),
        name="feed_both",
    )(place, lengths, tokens, ctx, cot, pool, vec)


def send_blocks(value, held, slot, first, place_ref, out_ref, sem):
    held[slot] = value.astype(jnp.bfloat16).reshape(D // BLK, BLK, D)
    for i in range(D // BLK):
        pltpu.make_async_copy(
            held.at[slot, i], out_ref.at[place_ref[first + i]], sem.at[slot]
        ).start()


def feed_grads_kernel(
    place_ref, ctx_ref, dbranch_ref, dinner_ref, mid_ref, act_ref, dfeed_ref, out_ref, held, sem
):
    step = pl.program_id(0)
    slot = lax.rem(step, 2)
    base = 3 * D // BLK

    @pl.when(step >= 2)
    def _():
        wait_whole(held.at[slot], sem.at[slot])

    first = base + step * (D // BLK)

    @pl.when(step == 0)
    def _():
        send_blocks(mm_tn(ctx_ref[...], dbranch_ref[...]), held, slot, first, place_ref, out_ref, sem)

    @pl.when((step >= 1) & (step <= CHUNKS))
    def _():
        send_blocks(mm_tn(dinner_ref[...], mid_ref[...]), held, slot, first, place_ref, out_ref, sem)

    @pl.when(step > CHUNKS)
    def _():
        send_blocks(mm_tn(act_ref[...], dfeed_ref[...]), held, slot, first, place_ref, out_ref, sem)

    @pl.when(step == 2 * CHUNKS)
    def _():
        wait_whole(held.at[slot], sem.at[slot])
        wait_whole(held.at[1 - slot], sem.at[1 - slot])


def feed_grads(place, places, ctx, d_branch, d_inner, mid, act, d_feed):
    total = ctx.shape[0]
    whole = pl.BlockSpec((total, D), lambda s, *_: (0, 0))
    return pl.pallas_call(
        feed_grads_kernel,
        grid_spec=pltpu.PrefetchScalarGridSpec(
            num_scalar_prefetch=1,
            grid=(1 + 2 * CHUNKS,),
            in_specs=[
                whole,
                whole,
                pl.BlockSpec((total, D), lambda s, *_: (0, jnp.clip(s - 1, 0, CHUNKS - 1))),
                whole,
                pl.BlockSpec((total, D), lambda s, *_: (0, jnp.clip(s - 1 - CHUNKS, 0, CHUNKS - 1))),
                whole,
            ],
            out_specs=pl.BlockSpec(memory_space=pl.ANY),
            scratch_shapes=[
                pltpu.VMEM((2, D // BLK, BLK, D), jnp.bfloat16),
                pltpu.SemaphoreType.DMA((2,)),
            ],
        ),
        out_shape=jax.ShapeDtypeStruct((places, BLK, D), jnp.bfloat16),
        compiler_params=pltpu.CompilerParams(vmem_limit_bytes=48 * MIB),
        cost_estimate=pl.CostEstimate(
            flops=4 * total * D * FF + 2 * total * D * D,
            bytes_accessed=total * (8 * D + 4 * FF) + 4 * FF * D,
            transcendentals=0,
        ),
        name="feed_grads",
    )(place, ctx, d_branch, d_inner, mid, act, d_feed)


def attend_back_kernel(
    place_w_ref, place_ref, lengths_ref, tokens_ref, q_ref, k_ref, v_ref, ctx_ref, dctx_ref, lse_ref, dres_ref, pool_ref, held_in,
    ingrad_ref, vec_ref, out_ref,
    w_scr, dq_scr, dk_scr, dv_scr, total_scr, held, sem, w_sem,
):
    seq = pl.program_id(0)
    last = pl.num_programs(0) - 1
    rows = tokens_ref.shape[0]

    @pl.when(seq == 0)
    def _():
        load_blocks(pool_ref, place_w_ref, 0, w_scr, w_sem)
        vec_ref[...] = jnp.zeros_like(vec_ref)

    key = lax.broadcasted_iota(jnp.int32, (rows, 1), 0)
    bias = jnp.where(key < lengths_ref[seq], 0.0, MASKED)

    def pair(p, _):
        cols, d_query, d_key, d_value = back_pair(q_ref, k_ref, v_ref, ctx_ref, dctx_ref, lse_ref, 0, p, bias)
        dq_scr[:, cols] = d_query
        dk_scr[:, cols] = d_key
        dv_scr[:, cols] = d_value
        return 0

    lax.fori_loop(0, PAIRS, pair, 0)

    @pl.when(seq == 0)
    def _():
        wait_whole(w_scr, w_sem)

    dq, dk, dv = dq_scr[...], dk_scr[...], dv_scr[...]
    vec_ref[0:1, :] += jnp.sum(dq.astype(jnp.float32), axis=0, keepdims=True)
    vec_ref[1:2, :] += jnp.sum(dv.astype(jnp.float32), axis=0, keepdims=True)
    ingrad = dres_ref[...] + mm_nt(dq, w_scr[0:D, :])
    ingrad += mm_nt(dk, w_scr[D : 2 * D, :])
    ingrad += mm_nt(dv, w_scr[2 * D :, :])
    ingrad_ref[...] = ingrad.astype(jnp.bfloat16)
    tokens = tokens_ref[...]
    for i, right in enumerate((dq, dk, dv)):
        part = slice(i * D, (i + 1) * D)

        @pl.when(seq == 0)
        def _():
            total_scr[part, :] = mm_tn(tokens, right)

        @pl.when(seq > 0)
        def _():
            total_scr[part, :] += mm_tn(tokens, right)

    @pl.when(seq == last)
    def _():
        for i in range(3):
            send_blocks(total_scr[i * D : (i + 1) * D, :], held, i, i * (D // BLK), place_ref, out_ref, sem)
        for i in range(3):
            wait_whole(held.at[i], sem.at[i])


def attend_back(place_w, place, lengths, tokens, q, k, v, ctx, d_ctx, lse, d_res, pool, held):
    seqs, rows, _ = tokens.shape
    flat = tokens.reshape(seqs * rows, D)
    row_spec = pl.BlockSpec((rows, D), lambda s, *_: (s, 0))
    any_spec = pl.BlockSpec(memory_space=pl.ANY)
    return pl.pallas_call(
        attend_back_kernel,
        grid_spec=pltpu.PrefetchScalarGridSpec(
            num_scalar_prefetch=3,
            grid=(seqs,),
            in_specs=[row_spec] * 6
            + [pl.BlockSpec((1, 16, rows), lambda s, *_: (s, 0, 0)), row_spec, any_spec, any_spec],
            out_specs=[row_spec, pl.BlockSpec((8, D), lambda s, *_: (0, 0)), any_spec],
            scratch_shapes=[
                pltpu.VMEM((3 * D, D), jnp.bfloat16),
                pltpu.VMEM((rows, D), jnp.bfloat16),
                pltpu.VMEM((rows, D), jnp.bfloat16),
                pltpu.VMEM((rows, D), jnp.bfloat16),
                pltpu.VMEM((3 * D, D), jnp.float32),
                pltpu.VMEM((3, D // BLK, BLK, D), jnp.bfloat16),
                pltpu.SemaphoreType.DMA((3,)),
                pltpu.SemaphoreType.DMA,
            ],
        ),
        out_shape=[
            jax.ShapeDtypeStruct((seqs * rows, D), jnp.bfloat16),
            jax.ShapeDtypeStruct((8, D), jnp.float32),
            jax.ShapeDtypeStruct(held.shape, held.dtype),
        ],
        input_output_aliases={12: 2},
        compiler_params=pltpu.CompilerParams(vmem_limit_bytes=56 * MIB),
        cost_estimate=pl.CostEstimate(
            flops=12 * seqs * rows * D * D + 10 * seqs * rows * rows * D,
            bytes_accessed=20 * seqs * rows * D + 12 * D * D,
            transcendentals=seqs * rows * rows * H,
        ),
        name="attend_back",
    )(place_w, place, lengths, flat, q, k, v, ctx, d_ctx, lse, d_res, pool, held)


def adam_kernel(
    place_ref, has_ref, grad_a, grad_b, moment_ref, second_ref, master_ref,
    dres_ref, part_ref, rms_ref, vec_ref, vec_moment_ref, vec_second_ref, vec_master_ref,
    ingrad_out, rms_out, grad_out, moment_out, second_out, master_out,
    vec_out, vec_moment_out, vec_second_out, vec_master_out,
):
    step = pl.program_id(0)
    for j, grad_in in enumerate((grad_a, grad_b)):
        got = grad_in[0].astype(jnp.float32)
        gradient = jnp.where(has_ref[2 * step + j] > 0, got, jnp.zeros_like(got))
        grad_out[j] = gradient
        moment_out[j], second_out[j], master_out[j] = adam_step(
            gradient, moment_ref[j], second_ref[j], master_ref[j], matrix_rate
        )
    ingrad_out[...] = dres_ref[...] + part_ref[...].astype(jnp.float32)

    @pl.when(step == 0)
    def _():
        rms_out[...] = rms_ref[:, 0:2]
        gradient = vec_ref[0 : vec_out.shape[0], :]
        vec_out[...] = gradient
        vec_moment_out[...], vec_second_out[...], vec_master_out[...] = adam_step(
            gradient, vec_moment_ref[...], vec_second_ref[...], vec_master_ref[...], vector_rate
        )


def adam_all(place, has, reduced, moment, second, master, d_res, part, rms, vec, vec_moment, vec_second, vec_master):
    slots = master.shape[0]
    steps = slots // 2
    total = d_res.shape[0]
    pieces = 1
    while 2 * pieces <= steps:
        pieces *= 2
    pair = pl.BlockSpec((2, BLK, D), lambda s, *_: (s, 0, 0))
    rows = pl.BlockSpec((total // pieces, D), lambda s, *_: (jnp.minimum(s, pieces - 1), 0))

    def whole(shape):
        return pl.BlockSpec(shape, lambda s, *_: (0, 0))

    full = jax.ShapeDtypeStruct(master.shape, jnp.float32)
    vec_full = jax.ShapeDtypeStruct(vec_master.shape, jnp.float32)
    return pl.pallas_call(
        adam_kernel,
        grid_spec=pltpu.PrefetchScalarGridSpec(
            num_scalar_prefetch=2,
            grid=(steps,),
            in_specs=[
                pl.BlockSpec((1, BLK, D), lambda s, place, has: (place[2 * s], 0, 0)),
                pl.BlockSpec((1, BLK, D), lambda s, place, has: (place[2 * s + 1], 0, 0)),
            ]
            + [pair] * 3
            + [rows] * 2
            + [whole(rms.shape), whole(vec.shape)]
            + [whole(vec_master.shape)] * 3,
            out_specs=[rows, whole((rms.shape[0], 2))] + [pair] * 4 + [whole(vec_master.shape)] * 4,
        ),
        out_shape=[
            jax.ShapeDtypeStruct(d_res.shape, jnp.float32),
            jax.ShapeDtypeStruct((rms.shape[0], 2), jnp.float32),
        ]
        + [full] * 4
        + [vec_full] * 4,
        compiler_params=pltpu.CompilerParams(vmem_limit_bytes=60 * MIB),
        cost_estimate=pl.CostEstimate(
            flops=20 * slots * BLK * D, bytes_accessed=30 * slots * BLK * D, transcendentals=2 * slots * BLK * D
        ),
        name="adam_all",
    )(place, has, reduced, reduced, moment, second, master, d_res, part, rms, vec, vec_moment, vec_second, vec_master)


EARLY = 6
MIDDLE = 8
LATE = 10
FIRST = 10
LIST = EARLY + MIDDLE + LATE
HEAD_BLOCKS = 3 * D // BLK
MESH = pl.DeviceIdType.MESH


class Place:
    def __init__(self):
        dp = lax.axis_index("dp")
        self.z = lax.axis_index("seq")
        self.core = dp % 2
        x = (dp // 2) % 2
        y = dp // 4
        self.chip = dp // 2
        self.chip_x = 2 * y + 1 - x
        self.chip_y = 2 * (1 - y) + x
        self.chip_xy = 2 * (1 - y) + 1 - x
        self.to_core = {"dp": dp + 1 - 2 * self.core}
        self.to_x = {"dp": dp + 2 - 4 * x}
        self.to_y = {"dp": dp + 4 - 8 * y}
        z = self.z
        self.z_hops = (z + 1 - 2 * (z % 2), (z + 2) % 4, 3 - z)
        self.to_z = tuple({"seq": hop} for hop in self.z_hops)
        self.partners = (self.to_core, self.to_x, self.to_y) + self.to_z

    def meet(self):
        barrier = pltpu.get_barrier_semaphore()
        for partner in self.partners:
            pl.semaphore_signal(barrier, inc=1, device_id=partner, device_id_type=MESH)
        pl.semaphore_wait(barrier, len(self.partners))


class Sender:
    def __init__(self, send_sem, recv_sem):
        self.send_sem, self.recv_sem = send_sem, recv_sem

    def copy(self, k, src, dst, partner):
        return pltpu.make_async_remote_copy(
            src_ref=src,
            dst_ref=dst,
            send_sem=self.send_sem.at[k],
            recv_sem=self.recv_sem.at[k],
            device_id=partner,
            device_id_type=MESH,
        )


class Gather:
    def __init__(self, here, sender, first_sem, count, own, own_row, pool, row_of):
        self.here, self.sender, self.k, self.n = here, sender, first_sem, count
        self.own, self.own_row, self.pool, self.row_of = own, own_row, pool, row_of
        self.half = count * BLK // 2

    def link(self, name):
        here, half = self.here, self.half

        def own(part):
            return self.own.at[pl.ds(self.own_row + part * half, half)]

        def piece(chip, part):
            return self.pool.at[pl.ds(self.row_of(chip, here.core) + part * half, half)]

        def whole(chip):
            return self.pool.at[pl.ds(self.row_of(chip, here.core), 2 * half)]

        order = ("x0", "x1", "y1", "y0", "y_on", "x_on", "share_x", "share_y", "share_xy")
        src, dst, partner = {
            "x0": lambda: (own(0), piece(here.chip, 0), here.to_x),
            "x1": lambda: (own(1), piece(here.chip, 1), here.to_x),
            "y1": lambda: (own(1), piece(here.chip, 1), here.to_y),
            "y0": lambda: (own(0), piece(here.chip, 0), here.to_y),
            "y_on": lambda: (piece(here.chip_x, 0), piece(here.chip_x, 0), here.to_y),
            "x_on": lambda: (piece(here.chip_y, 1), piece(here.chip_y, 1), here.to_x),
            "share_x": lambda: (whole(here.chip_x), whole(here.chip_x), here.to_core),
            "share_y": lambda: (whole(here.chip_y), whole(here.chip_y), here.to_core),
            "share_xy": lambda: (whole(here.chip_xy), whole(here.chip_xy), here.to_core),
        }[name]()
        return self.sender.copy(self.k + order.index(name), src, dst, partner)

    def start(self):
        for name in ("x0", "y1", "x1", "y0"):
            self.link(name).start()

    def pass_on(self):
        self.link("x0").wait_recv()
        self.link("y_on").start()
        self.link("y1").wait_recv()
        self.link("x_on").start()

    def share_near(self):
        self.link("x1").wait_recv()
        self.link("share_x").start()
        self.link("y0").wait_recv()
        self.link("share_y").start()

    def sent(self):
        for name in ("x0", "y1", "x1", "y0", "y_on", "x_on"):
            self.link(name).wait_send()

    def share_far(self):
        self.link("y_on").wait_recv()
        self.link("x_on").wait_recv()
        self.link("share_xy").start()

    def finish(self):
        for name in ("share_x", "share_y", "share_xy"):
            self.link(name).wait_recv()

    def shared(self):
        for name in ("share_x", "share_y", "share_xy"):
            self.link(name).wait_send()


def front_kernel(
    place_ref, mine_ref, lengths_ref, vec_ref, master_in, tokens_in,
    pool, q_out, k_out, v_out, ctx_out, w_out, tok_out, ctx_split, lse_ref,
    stage, both, near, pack, w, tok, qs, ks, vs, cs,
    send_sem, recv_sem, load_sem,
):
    here = Place()
    z = here.z
    sender = Sender(send_sem, recv_sem)
    rows = SEQLEN
    own = tokens_in.shape[0] // 4
    part = tokens_in.shape[1]
    slots = master_in.shape[0]
    groups = 3
    group = slots // groups
    second = LIST - FIRST

    def local(src, dst, k):
        return pltpu.make_async_copy(src, dst, load_sem.at[k])

    loads = [
        local(master_in.at[pl.ds(g * group, group)], stage.at[pl.ds(g * group, group)], g) for g in range(groups)
    ]
    for load in loads:
        load.start()
    own_tokens = [
        local(tokens_in.at[own * z + s], tok.at[pl.ds(s * rows + part * z, part)], 3 + s) for s in range(own)
    ]
    for load in own_tokens:
        load.start()
    here.meet()
    swaps = [
        sender.copy(
            own * hop + s,
            tokens_in.at[own * here.z_hops[hop] + s],
            tok.at[pl.ds(s * rows + part * z, part)],
            here.to_z[hop],
        )
        for hop in range(3)
        for s in range(own)
    ]
    for swap in swaps:
        swap.start()
    trades = [
        sender.copy(
            6 + g,
            both.at[pl.ds(here.core * slots + g * group, group)],
            both.at[pl.ds(here.core * slots + g * group, group)],
            here.to_core,
        )
        for g in range(groups)
    ]
    for g in range(groups):
        loads[g].wait()

        def convert(i, _):
            both[here.core * slots + g * group + i] = stage[g * group + i].astype(jnp.bfloat16)
            return 0

        lax.fori_loop(0, group, convert, 0)
        trades[g].start()
    for trade in trades:
        trade.wait_recv()

    def fill_near(p, _):
        near[pl.ds((here.chip * FIRST + p) * BLK, BLK), :] = both[mine_ref[p]]
        return 0

    lax.fori_loop(0, FIRST, fill_near, 0)
    first = Gather(
        here, sender, 9, FIRST // 2, near, (here.chip * FIRST + here.core * (FIRST // 2)) * BLK, near,
        lambda chip, core: (chip * FIRST + core * (FIRST // 2)) * BLK,
    )
    then = Gather(
        here, sender, 18, second // 2, pack, here.core * (second // 2) * BLK, pool,
        lambda chip, core: (chip * LIST + FIRST + core * (second // 2)) * BLK,
    )
    first.start()

    def fill_pack(p, _):
        pack[pl.ds(p * BLK, BLK), :] = both[mine_ref[FIRST + p]]
        return 0

    lax.fori_loop(0, second, fill_pack, 0)
    own_second = local(pack, pool.at[pl.ds((here.chip * LIST + FIRST) * BLK, second * BLK)], 5)
    own_second.start()
    first.pass_on()
    first.share_near()
    first.sent()
    then.start()
    first.share_far()
    first.finish()

    def fill_w(b, _):
        at = place_ref[b]
        w[pl.ds(b * BLK, BLK), :] = near[pl.ds(((at // LIST) * FIRST + at % LIST) * BLK, BLK), :]
        return 0

    lax.fori_loop(0, HEAD_BLOCKS, fill_w, 0)
    keeps = [
        local(near.at[pl.ds(chip * FIRST * BLK, FIRST * BLK)], pool.at[pl.ds(chip * LIST * BLK, FIRST * BLK)], 6 + chip)
        for chip in range(4)
    ] + [local(w, w_out, 10)]
    for keep in keeps:
        keep.start()
    for load in own_tokens:
        load.wait()
    for swap in swaps:
        swap.wait_recv()
    keep_tok = local(tok, tok_out, 11)
    keep_tok.start()

    def send_ctx(s, hop):
        return sender.copy(
            27 + 3 * s + hop,
            cs.at[pl.ds(s * rows + part * here.z_hops[hop], part)],
            ctx_split.at[own * z + s],
            here.to_z[hop],
        )

    def keep_own(s):
        at = pl.ds(s * rows, rows)
        return [local(ref.at[at], out.at[at], 12 + k) for k, (ref, out) in enumerate(((qs, q_out), (ks, k_out), (vs, v_out), (cs, ctx_out)))] + [
            local(cs.at[pl.ds(s * rows + part * z, part)], ctx_split.at[own * z + s], 16)
        ]

    key = lax.broadcasted_iota(jnp.int32, (rows, 1), 0)

    def sequence(s, _):
        at = pl.ds(pl.multiple_of(s * rows, rows), rows)
        values = tok[at, :]
        qs[at, :] = ((mm(values, w[0:D, :]) + vec_ref[0:1, :]).astype(jnp.bfloat16) * 0.125).astype(jnp.bfloat16)
        ks[at, :] = mm(values, w[D : 2 * D, :]).astype(jnp.bfloat16)
        vs[at, :] = (mm(values, w[2 * D :, :]) + vec_ref[1:2, :]).astype(jnp.bfloat16)
        bias = jnp.where(key < lengths_ref[own * z + s], 0.0, MASKED)

        def pair(p, _):
            forward_pair(qs.at[at], ks.at[at], vs.at[at], cs.at[at], lse_ref, s, p, bias)
            return 0

        lax.fori_loop(0, PAIRS, pair, 0)
        for hop in range(3):
            send_ctx(s, hop).start()

        @pl.when(s > 0)
        def _():
            for keep in keep_own(s - 1):
                keep.wait()

        for keep in keep_own(s):
            keep.start()

        @pl.when(s == 0)
        def _():
            then.pass_on()

        return 0

    lax.fori_loop(0, own, sequence, 0)
    then.share_near()
    then.share_far()
    then.sent()
    then.finish()
    for keep in keep_own(own - 1) + keeps + [keep_tok, own_second]:
        keep.wait()
    for s in range(own):
        for hop in range(3):
            send_ctx(s, hop).wait_recv()
            send_ctx(s, hop).wait_send()
    for copy in swaps + trades:
        copy.wait_send()
    first.shared()
    then.shared()


def front(place, mine, lengths, vec, master, tokens):
    seqs, part, _ = tokens.shape
    total = seqs * part
    own = total // SEQLEN
    any_spec = pl.BlockSpec(memory_space=pl.ANY)
    vmem = pl.BlockSpec(memory_space=pltpu.VMEM)
    smem = pl.BlockSpec(memory_space=pltpu.SMEM)
    low = jnp.bfloat16
    slots = master.shape[0]
    flat = jax.ShapeDtypeStruct((total, D), low)
    return pl.pallas_call(
        front_kernel,
        in_specs=[smem] * 3 + [vmem] + [any_spec] * 2,
        out_specs=[any_spec] * 8 + [vmem],
        out_shape=[
            jax.ShapeDtypeStruct((4 * LIST * BLK, D), low),
            flat,
            flat,
            flat,
            flat,
            jax.ShapeDtypeStruct((3 * D, D), low),
            flat,
            jax.ShapeDtypeStruct(tokens.shape, low),
            jax.ShapeDtypeStruct((own, 16, SEQLEN), jnp.float32),
        ],
        scratch_shapes=[
            pltpu.VMEM(master.shape, jnp.float32),
            pltpu.VMEM((2 * slots, BLK, D), low),
            pltpu.VMEM((4 * FIRST * BLK, D), low),
            pltpu.VMEM(((LIST - FIRST) * BLK, D), low),
            pltpu.VMEM((3 * D, D), low),
        ]
        + [pltpu.VMEM((total, D), low)] * 5
        + [
            pltpu.SemaphoreType.DMA((33,)),
            pltpu.SemaphoreType.DMA((33,)),
            pltpu.SemaphoreType.DMA((17,)),
        ],
        compiler_params=pltpu.CompilerParams(
            vmem_limit_bytes=60 * MIB, collective_id=2, has_side_effects=True
        ),
        cost_estimate=pl.CostEstimate(
            flops=6 * total * D * D + 4 * total * SEQLEN * D,
            bytes_accessed=40 * total * D + 8 * slots * BLK * D,
            transcendentals=total * SEQLEN * H,
        ),
        name="front",
    )(place, mine, lengths, vec, master, tokens)


def add_rows(out_ref, out_row, terms, count, step=64):
    def body(i, _):
        value = None
        for ref, row in terms:
            part = ref[pl.ds(row + i * step, step), :].astype(jnp.float32)
            value = part if value is None else value + part
        out_ref[pl.ds(out_row + i * step, step), :] = value.astype(jnp.bfloat16)
        return 0

    lax.fori_loop(0, count // step, body, 0)


class Reduce:
    def __init__(self, here, sender, first_sem, count, first, column, blk_ref, grad, pack, buffers, red):
        self.here, self.sender, self.k = here, sender, first_sem
        self.n, self.first, self.blk, self.grad = count, first, blk_ref, grad
        self.acc, self.rx, self.ry, self.r2, self.z1, self.z2, self.fin = buffers
        self.red = red
        self.half = count * BLK // 2
        self.size = count * BLK
        self.cols = pl.ds(column, self.fin.shape[1])
        self.pack = pack.at[pl.ds(0, 4 * self.size), self.cols]

    def rows(self, ref, chip, half):
        return ref.at[pl.ds(chip * self.size + half * self.half, self.half)]

    def link(self, name):
        here, k, acc = self.here, self.k, self.acc
        keep = (here.z % 2) * self.half
        other = (1 - here.z % 2) * self.half
        mine = here.chip * self.size
        fin_keep = self.fin.at[pl.ds(keep, self.half)]
        order = ("core", "x_far", "x_near", "y_far", "y_near", "y_on", "x_on", "z_half", "z_far", "z_back", "share")
        src, dst, partner = {
            "core": lambda: (self.pack, acc, here.to_core),
            "x_far": lambda: (self.rows(acc, here.chip_xy, 0), self.rx.at[1], here.to_x),
            "x_near": lambda: (self.rows(acc, here.chip_x, 0), self.rx.at[0], here.to_x),
            "y_far": lambda: (self.rows(acc, here.chip_xy, 1), self.ry.at[1], here.to_y),
            "y_near": lambda: (self.rows(acc, here.chip_y, 1), self.ry.at[0], here.to_y),
            "y_on": lambda: (self.rows(acc, here.chip_y, 0), self.r2.at[0], here.to_y),
            "x_on": lambda: (self.rows(acc, here.chip_x, 1), self.r2.at[1], here.to_x),
            "z_half": lambda: (acc.at[pl.ds(mine + other, self.half)], self.z1, here.to_z[0]),
            "z_far": lambda: (acc.at[pl.ds(mine + keep, self.half)], self.z2, here.to_z[1]),
            "z_back": lambda: (fin_keep, fin_keep, here.to_z[0]),
            "share": lambda: (self.fin, self.result(), here.to_core),
        }[name]()
        return self.sender.copy(k + order.index(name), src, dst, partner)

    def result(self):
        return self.red.at[pl.ds((self.first + self.here.core * self.n) * BLK, self.size), self.cols]

    def start_core(self):
        here, n = self.here, self.n

        def body(t, _):
            entry = (t // n) * LIST + self.first + (1 - here.core) * n + t % n
            self.pack[pl.ds(t * BLK, BLK), :] = self.grad[self.blk[entry], :, self.cols]
            return 0

        lax.fori_loop(0, 4 * n, body, 0)
        self.link("core").start()

    def add_own(self, chip):
        here, n = self.here, self.n

        def body(i, _):
            entry = chip * LIST + self.first + here.core * n + i
            rows = pl.ds(chip * self.size + i * BLK, BLK)
            mine = self.grad[self.blk[entry], :, self.cols].astype(jnp.float32)
            self.acc[rows, :] = (self.acc[rows, :].astype(jnp.float32) + mine).astype(jnp.bfloat16)
            return 0

        lax.fori_loop(0, n, body, 0)

    def start_plane(self):
        here = self.here
        self.link("core").wait_recv()
        self.add_own(here.chip_xy)
        self.link("x_far").start()
        self.link("y_far").start()
        self.add_own(here.chip_x)
        self.add_own(here.chip_y)
        self.link("x_near").start()
        self.link("y_near").start()
        self.add_own(here.chip)

    def pass_plane(self):
        here = self.here
        self.link("x_far").wait_recv()
        at = here.chip_y * self.size
        add_rows(self.acc, at, ((self.acc, at), (self.rx.at[1], 0)), self.half)
        self.link("y_on").start()
        self.link("y_far").wait_recv()
        at = here.chip_x * self.size + self.half
        add_rows(self.acc, at, ((self.acc, at), (self.ry.at[1], 0)), self.half)
        self.link("x_on").start()

    def start_z(self):
        here = self.here
        mine = here.chip * self.size
        self.link("x_near").wait_recv()
        self.link("y_on").wait_recv()
        add_rows(self.acc, mine, ((self.acc, mine), (self.rx.at[0], 0), (self.r2.at[0], 0)), self.half)
        self.link("y_near").wait_recv()
        self.link("x_on").wait_recv()
        low = mine + self.half
        add_rows(self.acc, low, ((self.acc, low), (self.ry.at[0], 0), (self.r2.at[1], 0)), self.half)
        self.link("z_half").start()

    def far_z(self):
        here = self.here
        keep = here.chip * self.size + (here.z % 2) * self.half
        self.link("z_half").wait_recv()
        add_rows(self.acc, keep, ((self.acc, keep), (self.z1, 0)), self.half)
        self.link("z_far").start()

    def back_z(self):
        here = self.here
        keep = (here.z % 2) * self.half
        self.link("z_far").wait_recv()
        add_rows(self.fin, keep, ((self.acc, here.chip * self.size + keep), (self.z2, 0)), self.half)
        self.link("z_back").start()

    def share(self, local_sem):
        red = self.result()
        self.link("z_back").wait_recv()
        self.link("z_back").wait_send()
        self.link("share").start()
        pltpu.make_async_copy(self.fin, red, local_sem).start()

    def finish(self, local_sem):
        red = self.result()
        self.link("share").wait_recv()
        pltpu.make_async_copy(self.fin, red, local_sem).wait()
        for name in ("core", "x_far", "x_near", "y_far", "y_near", "y_on", "x_on", "z_half", "z_far", "share"):
            if name != "core" or self.first >= EARLY + MIDDLE:
                self.link(name).wait_send()


def back_pair(q_ref, k_ref, v_ref, ctx_ref, do_ref, lse_ref, seq, p, bias):
    rows = q_ref.shape[0]
    cols = pl.ds(pl.multiple_of(p * LANES, LANES), LANES)
    row8 = lax.broadcasted_iota(jnp.int32, (16, rows), 0)

    def extra_rows(lead, row):
        one, two, three = (part.astype(jnp.float32) for part in split3(row))
        return jnp.where(
            row8 == 0, lead, jnp.where(row8 == 1, one, jnp.where(row8 == 2, two, jnp.where(row8 == 3, three, 0.0)))
        )

    q2, k2, v2, do2 = q_ref[:, cols], k_ref[:, cols], v_ref[:, cols], do_ref[:, cols]
    q2t, k2t, do2t = q2.T, k2.T, do2.T
    prod = do2t.astype(jnp.float32) * ctx_ref[:, cols].T.astype(jnp.float32)
    dq_parts = []
    d_key = jnp.zeros((rows, LANES), jnp.float32)
    d_value = jnp.zeros((rows, LANES), jnp.float32)
    for half in range(2):
        head = slice(half * DH, half * DH + DH)
        inside, spare = spare_lanes(rows, half, bias)
        zero = jnp.zeros_like(k2)
        lse = lse_ref[seq, pl.ds(2 * p + half, 1), :]
        delta = jnp.sum(prod[head], axis=0, keepdims=True)
        scores = mm(jnp.where(inside, k2, spare), beside(q2t[head], extra_rows(1.0, -lse), half))
        probs = jnp.exp(scores)
        d_probs = mm(jnp.where(inside, v2, spare), beside(do2t[head], extra_rows(0.0, -delta), half))
        d_scores = (probs * d_probs).astype(jnp.bfloat16)
        d_value += mm(probs.astype(jnp.bfloat16), jnp.where(inside, do2, zero))
        d_key += mm(d_scores, jnp.where(inside, q2, zero))
        dq_parts.append(mm(k2t[head], d_scores))
    d_query = jnp.concatenate(dq_parts, axis=0).T * 0.125
    return cols, d_query.astype(jnp.bfloat16), d_key.astype(jnp.bfloat16), d_value.astype(jnp.bfloat16)


def tail_kernel(
    blk_ref, lengths_ref, vec_in, squares_in, lse_ref,
    dctx_in, ctx_split, dbranch, dinner, mid, act, dfeed, tok_in, q_in, k_in, v_in, ctx_in, w_in,
    red, ingrad, vec_out, rms_out,
    grad, pack, d3, att, tok, w, *rest,
):
    here = Place()
    z = here.z
    phase_buffers = [rest[7 * i : 7 * i + 7] for i in range(4)]
    vec_src, vec_land, rms_src, rms_land, send_sem, recv_sem, load_sem = rest[28:]
    sender = Sender(send_sem, recv_sem)
    rows = SEQLEN
    own = dctx_in.shape[0] // 4
    part = dctx_in.shape[1]
    total = own * rows
    wide = D // 2

    def local(src, dst, k):
        return pltpu.make_async_copy(src, dst, load_sem.at[k])

    first_loads = (
        local(ctx_split, att.at[2], 0),
        local(dinner.at[:, pl.ds(0, D)], att.at[3], 1),
        local(dbranch, d3.at[0], 2),
        local(mid, d3.at[1], 3),
        local(dfeed, d3.at[2], 4),
        local(q_in, att.at[0], 5),
        local(k_in, att.at[1], 6),
        local(tok_in, tok, 7),
        local(w_in, w, 10),
    )
    for load in first_loads:
        load.start()
    here.meet()

    def swap(half, s, hop):
        cols = pl.ds(half * wide, wide)
        return sender.copy(
            6 * half + 3 * s + hop,
            dctx_in.at[own * here.z_hops[hop] + s, :, cols],
            att.at[4, pl.ds(s * rows + part * z, part), cols],
            here.to_z[hop],
        )

    swaps = [[swap(half, s, hop) for s in range(own) for hop in range(3)] for half in range(2)]
    own_swaps = [local(dctx_in.at[own * z + s], att.at[4, pl.ds(s * rows + part * z, part)], 8 + s) for s in range(own)]
    for copy in swaps[0] + own_swaps:
        copy.start()
    for load in first_loads[2:5]:
        load.wait()

    early, middle = (
        Reduce(here, sender, 24 + 11 * i, count // 2, first, 0, blk_ref, grad, pack, phase_buffers[i], red)
        for i, (count, first) in enumerate(((EARLY, 0), (MIDDLE, EARLY)))
    )
    late = [
        Reduce(here, sender, 46 + 11 * i, LATE // 2, EARLY + MIDDLE, i * wide, blk_ref, grad, pack, phase_buffers[2 + i], red)
        for i in range(2)
    ]

    def grads(step, _):
        slot = 2 + step % 2
        held = att.at[slot]
        pltpu.make_async_copy(held, held, load_sem.at[step % 2]).wait()
        value = mm_tn(att[slot], d3[(step + 3) // 4])
        grad[pl.ds(HEAD_BLOCKS + step * (D // BLK), D // BLK)] = value.astype(jnp.bfloat16).reshape(D // BLK, BLK, D)

        @pl.when(step < CHUNKS - 1)
        def _():
            local(dinner.at[:, pl.ds((step + 1) * D, D)], held, step % 2).start()

        @pl.when((step >= CHUNKS - 1) & (step < 2 * CHUNKS - 1))
        def _():
            local(act.at[:, pl.ds((step - CHUNKS + 1) * D, D)], held, step % 2).start()

        @pl.when(step == CHUNKS)
        def _():
            early.start_core()

        @pl.when(step == CHUNKS + 2)
        def _():
            early.start_plane()

        @pl.when(step == CHUNKS + 3)
        def _():
            for copy in swaps[0]:
                copy.wait_send()
            for copy in swaps[1]:
                copy.start()

        return 0

    grad[0:HEAD_BLOCKS] = jnp.zeros((HEAD_BLOCKS, BLK, D), jnp.bfloat16)
    lax.fori_loop(0, 1 + 2 * CHUNKS, grads, 0)
    more_loads = (local(v_in, att.at[2], 0), local(ctx_in, att.at[3], 1))
    for load in more_loads:
        load.start()
    early.link("core").wait_send()
    middle.start_core()
    for load in first_loads[5:] + tuple(own_swaps) + more_loads:
        load.wait()
    for copy in swaps[0]:
        copy.wait_recv()

    key = lax.broadcasted_iota(jnp.int32, (rows, 1), 0)

    def head_grads(half):
        cols = pl.ds(half * wide, wide)
        for block, which in ((0, 1), (6, 2), (12, 0)):
            value = mm_tn(tok[...], d3[which, :, cols]).astype(jnp.bfloat16)
            grad[block : block + 6, :, cols] = value.reshape(D // BLK, BLK, wide)

    def send_ingrad(s, hop):
        return sender.copy(
            68 + 3 * s + hop,
            att.at[0, pl.ds(s * rows + part * here.z_hops[hop], part)],
            ingrad.at[own * z + s],
            here.to_z[hop],
        )

    def own_ingrad(s):
        return local(att.at[0, pl.ds(s * rows + part * z, part)], ingrad.at[own * z + s], 11 + s)

    def input_gradient(s):
        at = pl.ds(s * rows, rows)
        value = mm_nt(d3[1, at, :], w[0:D, :])
        value += mm_nt(d3[2, at, :], w[D : 2 * D, :])
        value += mm_nt(d3[0, at, :], w[2 * D :, :])
        att[0, at, :] = value.astype(jnp.bfloat16)
        for hop in range(3):
            send_ingrad(s, hop).start()
        own_ingrad(s).start()

    group = PAIRS // 2

    def pair_step(i, _):
        s = (i // group) % own
        p = (i // (own * group)) * group + i % group
        bias = jnp.where(key < lengths_ref[own * z + s], 0.0, MASKED)
        at = pl.ds(pl.multiple_of(s * rows, rows), rows)
        cols, d_query, d_key, d_value = back_pair(*(att.at[k, at] for k in range(5)), lse_ref, s, p, bias)
        d3[1, at, cols] = d_query
        d3[2, at, cols] = d_key
        d3[0, at, cols] = d_value

        @pl.when(i == 0)
        def _():
            early.pass_plane()

        @pl.when(i == 2)
        def _():
            middle.start_plane()

        @pl.when(i == 4)
        def _():
            early.start_z()

        @pl.when(i == 5)
        def _():
            head_grads(0)
            middle.link("core").wait_send()
            late[0].start_core()
            for copy in swaps[1]:
                copy.wait_recv()

        @pl.when(i == 6)
        def _():
            middle.pass_plane()
            early.far_z()

        @pl.when(i == 8)
        def _():
            late[0].start_plane()
            input_gradient(0)

        @pl.when(i == 11)
        def _():
            middle.start_z()
            early.back_z()

        return 0

    lax.fori_loop(0, own * PAIRS, pair_step, 0)

    head_grads(1)
    late[1].start_core()
    vec_src[0] = vec_in[...]
    vec_src[0, 0:1, :] = jnp.sum(d3[1].astype(jnp.float32), axis=0, keepdims=True)
    vec_src[0, 1:2, :] = jnp.sum(d3[0].astype(jnp.float32), axis=0, keepdims=True)
    for i in range(squares_in.shape[0]):
        sums = jnp.sum(squares_in[i], axis=-1, keepdims=True)
        rms_src[0, 8 * i : 8 * i + 8, :] = jnp.broadcast_to(sums, (8, LANES))
    ways = (here.to_z[0], here.to_z[1], here.to_core, here.to_x, here.to_y)
    vec_copies = [sender.copy(12 + w, vec_src.at[w], vec_land.at[w], way) for w, way in enumerate(ways)]
    rms_copies = [sender.copy(17 + w, rms_src.at[w], rms_land.at[w], ways[w]) for w in range(2)]

    def vec_step(w):
        if w > 0:
            vec_copies[w - 1].wait_recv()
            after = vec_src[w - 1] + vec_land[w - 1]
            if w < len(ways):
                vec_src[w] = after
            else:
                vec_out[...] = after
        if w < len(ways):
            vec_copies[w].start()
        if 0 < w <= 2:
            rms_copies[w - 1].wait_recv()
            after = rms_src[w - 1] + rms_land[w - 1]
            if w < 2:
                rms_src[w] = after
            else:
                lane = lax.broadcasted_iota(jnp.int32, (1, LANES), 1)
                tiles = squares_in.shape[0]
                each = dctx_in.shape[0] // tiles
                for n in range(dctx_in.shape[0]):
                    row = 8 * (n // each) + 2 * (n % each)
                    sums = jnp.where(lane == 0, after[row : row + 1], after[row + 1 : row + 2])
                    rms_out[n : n + 1, :] = jnp.sqrt(sums / (lengths_ref[n].astype(jnp.float32) * D))
        if w < 2:
            rms_copies[w].start()

    late[0].pass_plane()
    vec_step(0)
    late[1].start_plane()
    middle.far_z()
    input_gradient(1)
    vec_step(1)
    late[1].pass_plane()
    late[0].start_z()
    early.share(load_sem.at[13])
    vec_step(2)
    late[0].far_z()
    late[1].start_z()
    vec_step(3)
    late[1].far_z()
    middle.back_z()
    late[0].back_z()
    vec_step(4)
    middle.share(load_sem.at[14])
    late[0].share(load_sem.at[15])
    vec_step(5)
    late[1].back_z()
    late[1].share(load_sem.at[16])
    for i, phase in enumerate((early, middle, late[0], late[1])):
        phase.finish(load_sem.at[13 + i])
    for copy in swaps[1] + vec_copies + rms_copies:
        copy.wait_send()
    for s in range(own):
        own_ingrad(s).wait()
        for hop in range(3):
            send_ingrad(s, hop).wait_recv()
            send_ingrad(s, hop).wait_send()


def tail(blk, lengths, vec, squares, lse, d_ctx, ctx_split, d_branch, d_inner, mid, act, d_feed, tokens, q, k, v, ctx, w):
    total = tokens.shape[0]
    any_spec = pl.BlockSpec(memory_space=pl.ANY)
    vmem = pl.BlockSpec(memory_space=pltpu.VMEM)
    smem = pl.BlockSpec(memory_space=pltpu.SMEM)
    low = jnp.bfloat16
    sums = (8 * squares.shape[0], LANES)

    def phase(n, width):
        half = n * BLK // 2
        return [
            pltpu.VMEM((4 * n * BLK, width), low),
            pltpu.VMEM((2, half, width), low),
            pltpu.VMEM((2, half, width), low),
            pltpu.VMEM((2, half, width), low),
            pltpu.VMEM((half, width), low),
            pltpu.VMEM((half, width), low),
            pltpu.VMEM((n * BLK, width), low),
        ]

    return pl.pallas_call(
        tail_kernel,
        in_specs=[smem] * 2 + [vmem] * 3 + [any_spec] * 13,
        out_specs=[any_spec] * 2 + [vmem] * 2,
        out_shape=[
            jax.ShapeDtypeStruct((LIST * BLK, D), low),
            jax.ShapeDtypeStruct(d_ctx.shape, low),
            jax.ShapeDtypeStruct(vec.shape, jnp.float32),
            jax.ShapeDtypeStruct((d_ctx.shape[0], LANES), jnp.float32),
        ],
        scratch_shapes=[
            pltpu.VMEM((HEAD_BLOCKS + (D + 2 * FF) // BLK, BLK, D), low),
            pltpu.VMEM((2 * max(EARLY, MIDDLE, LATE) * BLK, D), low),
            pltpu.VMEM((3, total, D), low),
            pltpu.VMEM((5, total, D), low),
            pltpu.VMEM((total, D), low),
            pltpu.VMEM((3 * D, D), low),
        ]
        + phase(EARLY // 2, D)
        + phase(MIDDLE // 2, D)
        + phase(LATE // 2, D // 2)
        + phase(LATE // 2, D // 2)
        + [
            pltpu.VMEM((5,) + vec.shape, jnp.float32),
            pltpu.VMEM((5,) + vec.shape, jnp.float32),
            pltpu.VMEM((2,) + sums, jnp.float32),
            pltpu.VMEM((2,) + sums, jnp.float32),
            pltpu.SemaphoreType.DMA((74,)),
            pltpu.SemaphoreType.DMA((74,)),
            pltpu.SemaphoreType.DMA((17,)),
        ],
        compiler_params=pltpu.CompilerParams(
            vmem_limit_bytes=63 * MIB, collective_id=1, has_side_effects=True
        ),
        cost_estimate=pl.CostEstimate(
            flops=2 * total * D * (6 * D + 2 * FF) + 10 * total * SEQLEN * D,
            bytes_accessed=total * (24 * D + 4 * FF) + 8 * FF * D,
            transcendentals=total * SEQLEN * H,
        ),
        name="tail",
    )(blk, lengths, vec, squares, lse, d_ctx, ctx_split, d_branch, d_inner, mid, act, d_feed, tokens, q, k, v, ctx, w)


def tables_kernel(owner_ref, place_ref, mine_ref, block_ref, spot_ref, has_ref, fits_ref, *, slots):
    dp = lax.axis_index("dp")
    chip_slots = 2 * slots
    near_blocks = HEAD_BLOCKS + (D + FF) // BLK
    for ref in (mine_ref, block_ref, spot_ref, has_ref):
        for i in range(ref.shape[0]):
            ref[i] = 0

    def body(b, counts):
        listed, early, middle, late, bad = counts
        slot = owner_ref[b]
        chip = slot // chip_slots
        shift = 8 * chip
        one = jnp.left_shift(1, shift)

        def count(packed):
            return jnp.right_shift(packed, shift) & 255

        order = count(listed)
        n_early, n_middle, n_late = count(early), count(middle), count(late)
        body_block = b >= HEAD_BLOCKS
        in_early = body_block & (b < near_blocks) & (n_early < EARLY)
        in_middle = body_block & jnp.logical_not(in_early) & (n_middle < MIDDLE)
        in_late = jnp.logical_not(in_early | in_middle)
        spot = jnp.where(in_early, n_early, jnp.where(in_middle, EARLY + n_middle, EARLY + MIDDLE + n_late))
        wrong = (order >= LIST) | (spot >= LIST) | (jnp.logical_not(body_block) & (order >= FIRST))
        spot = jnp.minimum(spot, LIST - 1)
        place_ref[b] = chip * LIST + jnp.minimum(order, LIST - 1)
        block_ref[chip * LIST + spot] = b

        @pl.when(chip == dp // 2)
        def _():
            mine_ref[jnp.minimum(order, LIST - 1)] = slot - chip * chip_slots

            @pl.when(slot // slots == dp)
            def _():
                spot_ref[slot % slots] = spot
                has_ref[slot % slots] = 1

        return (
            listed + one,
            early + jnp.where(in_early, one, 0),
            middle + jnp.where(in_middle, one, 0),
            late + jnp.where(in_late, one, 0),
            bad | wrong.astype(jnp.int32),
        )

    zero = jnp.int32(0)
    counts = lax.fori_loop(0, owner_ref.shape[0], body, (zero,) * 5, unroll=4)
    fits_ref[0] = 1 - counts[4]


def tables(owner, slots):
    chips = lax.axis_size("dp") // 2
    smem = pl.BlockSpec(memory_space=pltpu.SMEM)
    sizes = (owner.shape[0], LIST, chips * LIST, slots, slots, 1)
    return pl.pallas_call(
        partial(tables_kernel, slots=slots),
        in_specs=[smem],
        out_specs=[smem] * len(sizes),
        out_shape=[jax.ShapeDtypeStruct((n,), jnp.int32) for n in sizes],
        name="tables",
    )(owner)


def general(tokens, cotangent, lengths, owner, master, vec_master):
    slot_local = master.shape[0]
    gathered = lax.all_gather(master.astype(jnp.bfloat16), "dp", axis=0, tiled=True)
    seq_place = lax.axis_index("seq")
    slot_total = slot_local * lax.axis_size("dp")
    tokens = to_whole(tokens, "seq")
    cotangent = to_whole(cotangent, "seq")
    seq_count, seq_len, width = tokens.shape
    token_count = seq_count * seq_len
    lengths = lax.dynamic_slice_in_dim(lengths, seq_place * seq_count, seq_count)
    q, k, v, ctx, lse, _ = attend(owner, lengths, tokens, gathered, vec_master)
    flat = tokens.reshape(token_count, D)
    _, mid, out, act, d_inner, d_feed, d_branch, d_res, d_ctx, vec_feed, squares = feed_both(
        owner, lengths, seq_len,
        flat, ctx, cotangent.reshape(token_count, D), gathered, vec_master,
    )
    held = feed_grads(owner, slot_total, ctx, d_branch, d_inner, mid, act, d_feed)
    ingrad, vec_attend, held = attend_back(
        owner, owner, lengths, tokens, q, k, v, ctx, d_ctx, lse, d_res, gathered, held
    )
    local_sums = jnp.sum(squares.reshape(seq_count, -1, 8, D)[:, :, :2], axis=(1, 3))
    own_rms = jnp.sqrt(local_sums / (lengths[:, None].astype(jnp.float32) * D))
    sublayer_rms = lax.all_gather(own_rms, "seq", axis=0, tiled=True)
    vec_local = jnp.concatenate([vec_attend[:2], vec_feed[2:12]], axis=0)
    vec_grad = lax.psum(vec_local, ("dp", "seq"))
    owned = lax.psum_scatter(held, "dp", scatter_dimension=0, tiled=True)
    reduced = lax.psum(owned, "seq")
    first_slot = lax.axis_index("dp") * slot_local
    slots = jnp.arange(slot_local, dtype=jnp.int32)
    has = jnp.any((first_slot + slots)[:, None] == owner[None, :], axis=1).astype(jnp.int32)
    whole = (seq_count, seq_len, D)
    return (
        to_split(out.reshape(whole), "seq"),
        jnp.zeros((token_count, D), jnp.float32),
        to_split(ingrad.reshape(whole), "seq").reshape(token_count, D),
        to_split(mid.reshape(whole), "seq").astype(jnp.float32),
        jnp.pad(sublayer_rms, ((0, 0), (0, LANES - 2))),
        jnp.pad(vec_grad, ((0, 4), (0, 0))),
        reduced,
        slots,
        has,
    )


def listed(tokens, cotangent, lengths, owner, master, vec_master, place, mine, block, spot, has):
    seqs, part, _ = tokens.shape
    total = seqs * part
    pool, q, k, v, ctx, w, whole, ctx_split, lse = front(
        place, mine, lengths, vec_master, master, tokens
    )
    ctx_split = ctx_split.reshape(total, D)
    wide_mid, mid, out, act, d_inner, d_feed, d_branch, d_res, d_ctx, vec_feed, squares = feed_both(
        place, lengths, part,
        tokens.reshape(total, D), ctx_split, cotangent.reshape(total, D), pool.reshape(-1, BLK, D), vec_master,
    )
    reduced, ingrad, vec_grad, rms = tail(
        block, lengths, vec_feed, squares, lse, d_ctx.reshape(seqs, part, D), ctx_split, d_branch, d_inner,
        mid, act, d_feed, whole, q, k, v, ctx, w,
    )
    return (
        out.reshape(tokens.shape),
        d_res,
        ingrad.reshape(total, D),
        wide_mid.reshape(tokens.shape),
        rms,
        vec_grad,
        reduced.reshape(LIST, BLK, D),
        spot,
        has,
    )


def per_device(
    tokens, cotangent, lengths, owner, master, moment, second, vec_master, vec_moment, vec_second
):
    slot_local = master.shape[0]
    given = (tokens, cotangent, lengths, owner, master, vec_master)
    if lax.axis_size("dp") == 8 and lax.axis_size("seq") == 4:
        place, mine, block, spot, has, fits = tables(owner, slot_local)

        def otherwise(*args):
            results = general(*args[:6])
            pad = ((0, LIST - slot_local), (0, 0), (0, 0))
            return results[:6] + (jnp.pad(results[6], pad),) + results[7:]

        results = lax.cond(fits[0] > 0, listed, otherwise, *given, place, mine, block, spot, has)
    else:
        results = general(*given)
    layer_out, d_res, ingrad, residual_mid, rms, vec_grad, reduced, spot, has = results
    updated = adam_all(
        spot, has, reduced, moment, second, master,
        d_res, ingrad, rms, vec_grad, vec_moment, vec_second, vec_master,
    )
    input_grad, sublayer_rms, slots, vectors = updated[0], updated[1], updated[2:6], updated[6:]
    return (layer_out, input_grad.reshape(tokens.shape), residual_mid, sublayer_rms, *slots, *vectors)


def solution(mesh):
    return jax.shard_map(
        per_device,
        mesh=mesh,
        in_specs=(
            P("dp", "seq", None),
            P("dp", "seq", None),
            P("dp"),
            P(),
            P("dp", None, None),
            P("dp", None, None),
            P("dp", None, None),
            P(),
            P(),
            P(),
        ),
        out_specs=(
            P("dp", "seq", None),
            P("dp", "seq", None),
            P("dp", "seq", None),
            P("dp", None),
            P("dp", None, None),
            P("dp", None, None),
            P("dp", None, None),
            P("dp", None, None),
            P(),
            P(),
            P(),
            P(),
        ),
        check_vma=False,
    )
```

time: 1390 us -> 358 us (0.26)
  waiting for transfers between devices: 900 us -> 0 us
  Pallas kernels: 0 us -> 335 us
  matrix products: 199 us -> 0 us
  local copies, waits for them, and re-layouts: 147 us -> 1.34 us
  other arithmetic: 56.9 us -> 0 us
  blocking collectives: 55.1 us -> 0 us
    ppermute x14 -> x0, waiting for transfers between devices: 379 us -> none  [passed_along(): return lax.ppermute(block, axis, route)]
    pallas_call x0 -> x5, Pallas kernels: none -> 335 us  [the longest x1 164 us: tail(): pl.pallas_call(tail_kernel, in_specs=[smem] * 2 + [vmem] * 3 + [any_spec]...]
    reduce_scatter x1 -> x0, waiting for transfers between devices: 316 us -> none  [per_device(): owned = lax.psum_scatter(slotted, 'dp', scatter_dimension=0, tiled=True)]
    dot_general x42 -> x0, matrix products: 199 us -> none  [the longest x1 34.3 us: per_device(): jnp.einsum('td,fd->tf', middle_low, w_up, preferred_element_type=jnp.floa...]
    all_gather x1 -> x0, waiting for transfers between devices: 140 us -> none  [per_device(): gathered = lax.all_gather(local_master, 'dp', axis=0, tiled=True)]
    psum x1 -> x0, waiting for transfers between devices: 65.1 us -> none  [per_device(): grad_pool = lax.psum(owned.astype(jnp.bfloat16), 'seq').astype(jnp.float32)]
    scatter x1 -> x0, local copies, waits for them, and re-layouts: 57.5 us -> none  [per_device(): jnp.zeros((slot_total, BLK, D), jnp.float32).at[owner].set(flat_grad)]
    psum x2 -> x0, blocking collectives: 55.1 us -> none  [the longest x1 43.1 us: per_device(): vec_grad = lax.psum(vec_local, ('dp', 'seq'))]
  transfers between devices with their start and end apart: 17 -> 0, of which waited for: 17 -> 0; matrix products, arithmetic and copies ran while one was open for 8% -> 0% of each run, Pallas kernels for 0% -> 0%
where the time goes in v1:
time: 358 us; the launch traced here: 354 us
  Pallas kernels  335 us (94%)
  between operations  14.9 us (4%)
    pallas_call x1, Pallas kernels, tail(): pl.pallas_call(tail_kernel, in_specs=[smem] * 2 + [vmem] * 3 + [any_spec]...  164 us
    pallas_call x1, Pallas kernels, front(): pl.pallas_call(front_kernel, in_specs=[smem] * 3 + [vmem] + [any_spec] *...  95.7 us
    pallas_call x1, Pallas kernels, feed_both(): pl.pallas_call(partial(feed_kernel, seq_rows=seq_rows), grid_spec=pltpu.P...  45.8 us
    pallas_call x1, Pallas kernels, adam_all(): pl.pallas_call(adam_kernel, grid_spec=pltpu.PrefetchScalarGridSpec(num_sc...  25.2 us

profile of v1, /device:TPU:0, one launch (start us, length us, event | category | flops | bytes accessed | tf_op | source)
XLA Modules:
  0.0 354.4 jit_solution(17774334403034796889)
XLA Ops:
  7.2 3.6 %tables.1 = (s32[72]{0:T(128)}, s32[24]{0:T(128)}, s32[96]{0:T(128)}, s32[18]{0:T(128)}, s32[18]{0:T(128)}, /*index=5*/s32[1]{0:T(128)}) custom-call(s32[72]{0:T(128)} %owner_ref.1), custom_call_target="tpu_custom_call" | custom-call | tf_op jit(solution)/shard_map/tables/pallas_call | solution.py:1503
  11.4 309.4 %conditional.1 = (bf16[8,128,768]{2,1,0:T(8,128)(2,1)}, f32[1024,768]{1,0:T(8,128)}, bf16[1024,768]{1,0:T(8,128)(2,1)}, f32[8,128,768]{2,1,0:T(8,128)}, f32[16,7...) conditional(s32[]{:T(128)} %bitcast.58, (s32[8]{0:T(128)}, ...), branch_computations={%region_0.7_spmd, %region_6.8_spmd} | conditional | flops 49143767040 | bytes 522747968 | solution.py:1597
  14.6 0.0 copy-start.10
  14.6 0.0 copy-start.12
  14.6 0.0 copy-start.19
  14.6 0.0 copy-start.26
  14.6 0.0 copy-start.27
  14.6 95.7 %front.1 = (bf16[12288,768]{1,0:T(8,128)(2,1)}, bf16[1024,768]{1,0:T(8,128)(2,1)}, bf16[1024,768]{1,0:T(8,128)(2,1)}, bf16[1024,768]{1,0:T(8,128)(2,1)}, bf16[10...) custom-call(s32[72]{0:T(128)} %get-tuple-element.57.place_ref, ...), custom_call_target="tpu_custom_call" | custom-call | flops 5234491392 | bytes 45613056 | tf_op jit(solution)/shard_map/cond/branch_1_fun/front/pallas_call | solution.py:916
  110.3 0.0 copy-done.10
  110.3 0.0 copy-done.12
  110.3 0.0 copy-done.19
  110.3 0.0 copy-done.26
  110.3 0.0 copy-done.27
  110.4 0.0 copy-start.28
  110.4 45.8 %feed_both.3 = (f32[1024,768]{1,0:T(8,128)}, bf16[1024,768]{1,0:T(8,128)(2,1)}, bf16[1024,768]{1,0:T(8,128)(2,1)}, bf16[1024,3072]{1,0:T(8,128)(2,1)}, bf16[1024...) custom-call(s32[72]{0:T(128)S(1)} %copy-done.27, ...), custom_call_target="tpu_custom_call" | custom-call | flops 21743271936 | bytes 53477376 | tf_op jit(solution)/shard_map/cond/branch_1_fun/feed_both/pallas_call | solution.py:346
  156.2 0.0 copy-done.28
  156.2 164.5 %tail.1 = (bf16[3072,768]{1,0:T(8,128)(2,1)}, bf16[8,128,768]{2,1,0:T(8,128)(2,1)}, f32[16,768]{1,0:T(8,128)}, f32[8,128]{1,0:T(8,128)S(1)}) custom-call(s32[96]{0:T(128)S(1)} %copy-done.28, s32[8]{0:T(128)S(1)} %copy-done.26, f32[16,768]{1,0:T(8,128)} %get-tuple-element.69.vec_in, f32[4,8,768]{2,1,0:T(8,128)} %get-tuple-element.70.squares_in, ...), custom_call_target="tpu_custom_call" | custom-call | flops 20937965568 | bytes 50331648 | tf_op jit(solution)/shard_map/cond/branch_1_fun/tail/pallas_call | solution.py:1404
  320.9 25.2 %adam_all.1 = (f32[1024,768]{1,0:T(8,128)}, f32[8,2]{1,0:T(8,128)}, f32[18,128,768]{2,1,0:T(8,128)}, f32[18,128,768]{2,1,0:T(8,128)}, f32[18,128,768]{2,1,0:T(8,...) custom-call(s32[18]{0:T(128)} %get-tuple-element.135.place_ref, ...), custom_call_target="tpu_custom_call" | custom-call | flops 35389440 | bytes 53084160 | tf_op jit(solution)/shard_map/adam_all/pallas_call | solution.py:586
  346.1 1.3 copy.44
Async XLA Ops:
  14.6 95.7 %copy-start.10 = (bf16[8,128,768]{2,1,0:T(8,128)(2,1)S(1)}, bf16[8,128,768]{2,1,0:T(8,128)(2,1)}, u32[]{:S(2)}) copy-start(bf16[8,128,768]{2,1,0:T(8,128)(2,1)} %get-tuple-element.59.tokens_in) | copy-start | bytes 4718596 | tf_op jit(solution)/shard_map/cond
  14.6 95.7 %copy-start.12 = (bf16[8,128,768]{2,1,0:T(8,128)(2,1)S(1)}, bf16[8,128,768]{2,1,0:T(8,128)(2,1)}, u32[]{:S(2)}) copy-start(bf16[8,128,768]{2,1,0:T(8,128)(2,1)} %get-tuple-element.64) | copy-start | bytes 4718596 | tf_op jit(solution)/shard_map/cond
  14.6 95.7 %copy-start.19 = (f32[12,768]{1,0:T(8,128)S(1)}, f32[12,768]{1,0:T(8,128)}, u32[]{:S(2)}) copy-start(f32[12,768]{1,0:T(8,128)} %get-tuple-element.61.vec_ref) | copy-start | bytes 110596 | tf_op jit(solution)/shard_map/cond
  14.6 95.7 %copy-start.26 = (s32[8]{0:T(128)S(1)}, s32[8]{0:T(128)}, u32[]{:S(2)}) copy-start(s32[8]{0:T(128)} %get-tuple-element.58.lengths_ref) | copy-start | bytes 100 | tf_op jit(solution)/shard_map/cond
  14.6 95.7 %copy-start.27 = (s32[72]{0:T(128)S(1)}, s32[72]{0:T(128)}, u32[]{:S(2)}) copy-start(s32[72]{0:T(128)} %get-tuple-element.57.place_ref) | copy-start | bytes 868 | tf_op jit(solution)/shard_map/cond
  110.4 45.8 %copy-start.28 = (s32[96]{0:T(128)S(1)}, s32[96]{0:T(128)}, u32[]{:S(2)}) copy-start(s32[96]{0:T(128)} %get-tuple-element.68.blk_ref) | copy-start | bytes 1156 | tf_op jit(solution)/shard_map/cond

commit v2 on v1

--- a/solution.py
+++ b/solution.py
@@ -296,17 +296,32 @@
     @pl.when(step == 0)
     def _():
         wait_whole(w_up, sem.at[1])
-        wait_whole(w_down, sem.at[2])
 
     feed = jnp.zeros((rows, D), jnp.float32) + vec_ref[3:4, :]
-    for c in range(CHUNKS):
-        part = slice(c * D, (c + 1) * D)
-        inner = mm_nt(mid_low, w_up[part, :]) + vec_ref[8 + c : 9 + c, :]
+    parts = [slice(c * D, (c + 1) * D) for c in range(CHUNKS)]
+
+    def up(c):
+        return mm_nt(mid_low, w_up[parts[c], :])
+
+    def bend(c, inner):
+        inner = inner + vec_ref[8 + c : 9 + c, :]
         dist, bell = gelu_parts(inner)
         act = (inner * dist).astype(jnp.bfloat16)
-        act_ref[:, part] = act
-        slope_scr[:, part] = dist + bell
-        feed += mm(act, w_down[part, :])
+        act_ref[:, parts[c]] = act
+        slope_scr[:, parts[c]] = dist + bell
+        return act
+
+    inner = up(0)
+
+    @pl.when(step == 0)
+    def _():
+        wait_whole(w_down, sem.at[2])
+
+    for c in range(CHUNKS):
+        after = up(c + 1) if c + 1 < CHUNKS else None
+        act = bend(c, inner)
+        feed += mm(act, w_down[parts[c], :])
+        inner = after
     square_sums(1, feed)
     hat2, scale2 = norm_stats(middle + feed)
     gain2 = vec_ref[6:7, :]
@@ -319,12 +334,14 @@
     dfeed_ref[...] = d_feed
     add_row(3, d_feed.astype(jnp.float32))
     d_mid = d_res2
+    d_act = mm_nt(d_feed, w_down[parts[0], :])
     for c in range(CHUNKS):
-        part = slice(c * D, (c + 1) * D)
-        d_inner = (mm_nt(d_feed, w_down[part, :]) * slope_scr[:, part]).astype(jnp.bfloat16)
-        dinner_ref[:, part] = d_inner
+        after = mm_nt(d_feed, w_down[parts[c + 1], :]) if c + 1 < CHUNKS else None
+        d_inner = (d_act * slope_scr[:, parts[c]]).astype(jnp.bfloat16)
+        dinner_ref[:, parts[c]] = d_inner
         add_row(8 + c, d_inner.astype(jnp.float32))
-        d_mid += mm(d_inner, w_up[part, :])
+        d_mid += mm(d_inner, w_up[parts[c], :])
+        d_act = after
     add_row(4, d_mid * hat1)
     add_row(5, d_mid)
     d_res1 = norm_back(d_mid, vec_ref[4:5, :], hat1, scale1)
@@ -335,7 +352,7 @@
     dctx_ref[...] = mm_nt(d_branch, w_out[...]).astype(jnp.bfloat16)
 
 
-def feed_both(place, lengths, seq_rows, tokens, ctx, cot, pool, vec, tile=256):
+def feed_both(place, lengths, seq_rows, tokens, ctx, cot, pool, vec, tile=512):
     total = tokens.shape[0]
     steps = total // tile
     row_spec = pl.BlockSpec((tile, D), lambda s, *_: (s, 0))
@@ -363,7 +380,7 @@
         out_shape=[jax.ShapeDtypeStruct((total, D), jnp.float32), low, low, wide, wide, low, low, jax.ShapeDtypeStruct((total, D), jnp.float32), low,
             jax.ShapeDtypeStruct((16, D), jnp.float32),
             jax.ShapeDtypeStruct((steps, 8, D), jnp.float32)],
-        compiler_params=pltpu.CompilerParams(vmem_limit_bytes=56 * MIB),
+        compiler_params=pltpu.CompilerParams(vmem_limit_bytes=62 * MIB),
         cost_estimate=pl.CostEstimate(
             flops=8 * total * D * FF + 4 * total * D * D,
             bytes_accessed=total * (16 * D + 4 * FF) + 12 * FF * D,
@@ -532,7 +549,7 @@
             jax.ShapeDtypeStruct(held.shape, held.dtype),
         ],
         input_output_aliases={12: 2},
-        compiler_params=pltpu.CompilerParams(vmem_limit_bytes=56 * MIB),
+        compiler_params=pltpu.CompilerParams(vmem_limit_bytes=62 * MIB),
         cost_estimate=pl.CostEstimate(
             flops=12 * seqs * rows * D * D + 10 * seqs * rows * rows * D,
             bytes_accessed=20 * seqs * rows * D + 12 * D * D,
@@ -680,7 +697,7 @@
         def whole(chip):
             return self.pool.at[pl.ds(self.row_of(chip, here.core), 2 * half)]
 
-        order = ("x0", "x1", "y1", "y0", "y_on", "x_on", "share_x", "share_y", "share_xy")
+        order = ("x0", "x1", "y1", "y0", "y_on", "x_on", "share_x", "share_y", "share_xy", "share_me")
         src, dst, partner = {
             "x0": lambda: (own(0), piece(here.chip, 0), here.to_x),
             "x1": lambda: (own(1), piece(here.chip, 1), here.to_x),
@@ -691,11 +708,14 @@
             "share_x": lambda: (whole(here.chip_x), whole(here.chip_x), here.to_core),
             "share_y": lambda: (whole(here.chip_y), whole(here.chip_y), here.to_core),
             "share_xy": lambda: (whole(here.chip_xy), whole(here.chip_xy), here.to_core),
+            "share_me": lambda: (
+                self.own.at[pl.ds(self.own_row, 2 * half)], whole(here.chip), here.to_core
+            ),
         }[name]()
         return self.sender.copy(self.k + order.index(name), src, dst, partner)
 
     def start(self):
-        for name in ("x0", "y1", "x1", "y0"):
+        for name in ("x0", "y1", "x1", "y0", "share_me"):
             self.link(name).start()
 
     def pass_on(self):
@@ -720,18 +740,18 @@
         self.link("share_xy").start()
 
     def finish(self):
-        for name in ("share_x", "share_y", "share_xy"):
+        for name in ("share_me", "share_x", "share_y", "share_xy"):
             self.link(name).wait_recv()
 
     def shared(self):
-        for name in ("share_x", "share_y", "share_xy"):
+        for name in ("share_me", "share_x", "share_y", "share_xy"):
             self.link(name).wait_send()
 
 
 def front_kernel(
     place_ref, mine_ref, lengths_ref, vec_ref, master_in, tokens_in,
     pool, q_out, k_out, v_out, ctx_out, w_out, tok_out, ctx_split, lse_ref,
-    stage, both, near, pack, w, tok, qs, ks, vs, cs,
+    stage, give, take, near, pack, w, tok, qs, ks, vs, cs,
     send_sem, recv_sem, load_sem,
 ):
     here = Place()
@@ -741,18 +761,13 @@
     own = tokens_in.shape[0] // 4
     part = tokens_in.shape[1]
     slots = master_in.shape[0]
-    groups = 3
-    group = slots // groups
     second = LIST - FIRST
 
     def local(src, dst, k):
         return pltpu.make_async_copy(src, dst, load_sem.at[k])
 
-    loads = [
-        local(master_in.at[pl.ds(g * group, group)], stage.at[pl.ds(g * group, group)], g) for g in range(groups)
-    ]
-    for load in loads:
-        load.start()
+    load_master = local(master_in, stage, 0)
+    load_master.start()
     own_tokens = [
         local(tokens_in.at[own * z + s], tok.at[pl.ds(s * rows + part * z, part)], 3 + s) for s in range(own)
     ]
@@ -771,48 +786,63 @@
     ]
     for swap in swaps:
         swap.start()
+    parts = (FIRST // 2, second // 2)
+    starts = (0, FIRST)
     trades = [
         sender.copy(
-            6 + g,
-            both.at[pl.ds(here.core * slots + g * group, group)],
-            both.at[pl.ds(here.core * slots + g * group, group)],
+            6 + i,
+            give.at[pl.ds(i * parts[0] * BLK, parts[i] * BLK)],
+            take.at[pl.ds(i * parts[0] * BLK, parts[i] * BLK)],
             here.to_core,
         )
-        for g in range(groups)
+        for i in range(2)
     ]
-    for g in range(groups):
-        loads[g].wait()
-
-        def convert(i, _):
-            both[here.core * slots + g * group + i] = stage[g * group + i].astype(jnp.bfloat16)
+    load_master.wait()
+
+    def held(entry):
+        return stage[jnp.clip(mine_ref[entry] - here.core * slots, 0, slots - 1)].astype(jnp.bfloat16)
+
+    for i in range(2):
+
+        def fill_give(p, _):
+            give[pl.ds((i * parts[0] + p) * BLK, BLK), :] = held(starts[i] + (1 - here.core) * parts[i] + p)
             return 0
 
-        lax.fori_loop(0, group, convert, 0)
-        trades[g].start()
-    for trade in trades:
-        trade.wait_recv()
+        lax.fori_loop(0, parts[i], fill_give, 0)
+        trades[i].start()
+
+    def own_block(i, p):
+        entry = starts[i] + here.core * parts[i] + p
+        traded = take[pl.ds((i * parts[0] + p) * BLK, BLK), :]
+        return jnp.where(mine_ref[entry] // slots == here.core, held(entry), traded)
+
+    trades[0].wait_recv()
 
     def fill_near(p, _):
-        near[pl.ds((here.chip * FIRST + p) * BLK, BLK), :] = both[mine_ref[p]]
+        near[pl.ds((here.chip * FIRST + here.core * parts[0] + p) * BLK, BLK), :] = own_block(0, p)
         return 0
 
-    lax.fori_loop(0, FIRST, fill_near, 0)
+    lax.fori_loop(0, parts[0], fill_near, 0)
     first = Gather(
-        here, sender, 9, FIRST // 2, near, (here.chip * FIRST + here.core * (FIRST // 2)) * BLK, near,
+        here, sender, 8, FIRST // 2, near, (here.chip * FIRST + here.core * (FIRST // 2)) * BLK, near,
         lambda chip, core: (chip * FIRST + core * (FIRST // 2)) * BLK,
     )
     then = Gather(
-        here, sender, 18, second // 2, pack, here.core * (second // 2) * BLK, pool,
+        here, sender, 18, second // 2, pack, 0, pool,
         lambda chip, core: (chip * LIST + FIRST + core * (second // 2)) * BLK,
     )
     first.start()
 
+    trades[1].wait_recv()
+
     def fill_pack(p, _):
-        pack[pl.ds(p * BLK, BLK), :] = both[mine_ref[FIRST + p]]
+        pack[pl.ds(p * BLK, BLK), :] = own_block(1, p)
         return 0
 
-    lax.fori_loop(0, second, fill_pack, 0)
-    own_second = local(pack, pool.at[pl.ds((here.chip * LIST + FIRST) * BLK, second * BLK)], 5)
+    lax.fori_loop(0, parts[1], fill_pack, 0)
+    own_second = local(
+        pack, pool.at[pl.ds((here.chip * LIST + FIRST + here.core * parts[1]) * BLK, parts[1] * BLK)], 5
+    )
     own_second.start()
     first.pass_on()
     first.share_near()
@@ -842,7 +872,7 @@
 
     def send_ctx(s, hop):
         return sender.copy(
-            27 + 3 * s + hop,
+            28 + 3 * s + hop,
             cs.at[pl.ds(s * rows + part * here.z_hops[hop], part)],
             ctx_split.at[own * z + s],
             here.to_z[hop],
@@ -930,15 +960,16 @@
         ],
         scratch_shapes=[
             pltpu.VMEM(master.shape, jnp.float32),
-            pltpu.VMEM((2 * slots, BLK, D), low),
+            pltpu.VMEM((LIST // 2 * BLK, D), low),
+            pltpu.VMEM((LIST // 2 * BLK, D), low),
             pltpu.VMEM((4 * FIRST * BLK, D), low),
-            pltpu.VMEM(((LIST - FIRST) * BLK, D), low),
+            pltpu.VMEM(((LIST - FIRST) // 2 * BLK, D), low),
             pltpu.VMEM((3 * D, D), low),
         ]
         + [pltpu.VMEM((total, D), low)] * 5
         + [
-            pltpu.SemaphoreType.DMA((33,)),
-            pltpu.SemaphoreType.DMA((33,)),
+            pltpu.SemaphoreType.DMA((34,)),
+            pltpu.SemaphoreType.DMA((34,)),
             pltpu.SemaphoreType.DMA((17,)),
         ],
         compiler_params=pltpu.CompilerParams(
@@ -953,16 +984,16 @@
     )(place, mine, lengths, vec, master, tokens)
 
 
-def add_rows(out_ref, out_row, terms, count, step=64):
+def add_rows(out_ref, out_row, terms, count, step=32):
     def body(i, _):
         value = None
         for ref, row in terms:
-            part = ref[pl.ds(row + i * step, step), :].astype(jnp.float32)
+            part = ref[pl.ds(pl.multiple_of(row + i * step, step), step), :]
             value = part if value is None else value + part
-        out_ref[pl.ds(out_row + i * step, step), :] = value.astype(jnp.bfloat16)
+        out_ref[pl.ds(pl.multiple_of(out_row + i * step, step), step), :] = value
         return 0
 
-    lax.fori_loop(0, count // step, body, 0)
+    lax.fori_loop(0, count // step, body, 0, unroll=2)
 
 
 class Reduce:
@@ -985,9 +1016,20 @@
         other = (1 - here.z % 2) * self.half
         mine = here.chip * self.size
         fin_keep = self.fin.at[pl.ds(keep, self.half)]
-        order = ("core", "x_far", "x_near", "y_far", "y_near", "y_on", "x_on", "z_half", "z_far", "z_back", "share")
+        order = (
+            "core_xy", "core_x", "core_y", "core_me", "x_far", "x_near", "y_far", "y_near",
+            "y_on", "x_on", "z_half", "z_far", "z_back", "share",
+        )
+
+        def across(chip):
+            rows = pl.ds(chip * self.size, self.size)
+            return self.pack.at[rows], acc.at[rows], here.to_core
+
         src, dst, partner = {
-            "core": lambda: (self.pack, acc, here.to_core),
+            "core_xy": lambda: across(here.chip_xy),
+            "core_x": lambda: across(here.chip_x),
+            "core_y": lambda: across(here.chip_y),
+            "core_me": lambda: across(here.chip),
             "x_far": lambda: (self.rows(acc, here.chip_xy, 0), self.rx.at[1], here.to_x),
             "x_near": lambda: (self.rows(acc, here.chip_x, 0), self.rx.at[0], here.to_x),
             "y_far": lambda: (self.rows(acc, here.chip_xy, 1), self.ry.at[1], here.to_y),
@@ -1006,38 +1048,47 @@
 
     def start_core(self):
         here, n = self.here, self.n
-
-        def body(t, _):
-            entry = (t // n) * LIST + self.first + (1 - here.core) * n + t % n
-            self.pack[pl.ds(t * BLK, BLK), :] = self.grad[self.blk[entry], :, self.cols]
-            return 0
-
-        lax.fori_loop(0, 4 * n, body, 0)
-        self.link("core").start()
+        chips = (here.chip_xy, here.chip_x, here.chip_y, here.chip)
+        for chip, name in zip(chips, ("core_xy", "core_x", "core_y", "core_me")):
+
+            def body(i, _):
+                block = self.blk[chip * LIST + self.first + (1 - here.core) * n + i]
+                self.pack[pl.ds(chip * self.size + i * BLK, BLK), :] = self.grad[block, :, self.cols]
+                return 0
+
+            lax.fori_loop(0, n, body, 0)
+            self.link(name).start()
+
+    def sent_core(self):
+        for name in ("core_xy", "core_x", "core_y", "core_me"):
+            self.link(name).wait_send()
 
     def add_own(self, chip):
         here, n = self.here, self.n
 
         def body(i, _):
             entry = chip * LIST + self.first + here.core * n + i
-            rows = pl.ds(chip * self.size + i * BLK, BLK)
-            mine = self.grad[self.blk[entry], :, self.cols].astype(jnp.float32)
-            self.acc[rows, :] = (self.acc[rows, :].astype(jnp.float32) + mine).astype(jnp.bfloat16)
+            block = self.blk[entry]
+            for piece in range(0, BLK, 32):
+                rows = pl.ds(pl.multiple_of(chip * self.size + i * BLK, BLK) + piece, 32)
+                self.acc[rows, :] = self.acc[rows, :] + self.grad[block, piece : piece + 32, self.cols]
             return 0
 
         lax.fori_loop(0, n, body, 0)
 
-    def start_plane(self):
-        here = self.here
-        self.link("core").wait_recv()
-        self.add_own(here.chip_xy)
+    def start_far(self):
+        self.link("core_xy").wait_recv()
+        self.add_own(self.here.chip_xy)
         self.link("x_far").start()
         self.link("y_far").start()
-        self.add_own(here.chip_x)
-        self.add_own(here.chip_y)
+
+    def start_near(self):
+        self.link("core_x").wait_recv()
+        self.add_own(self.here.chip_x)
         self.link("x_near").start()
+        self.link("core_y").wait_recv()
+        self.add_own(self.here.chip_y)
         self.link("y_near").start()
-        self.add_own(here.chip)
 
     def pass_plane(self):
         here = self.here
@@ -1053,6 +1104,8 @@
     def start_z(self):
         here = self.here
         mine = here.chip * self.size
+        self.link("core_me").wait_recv()
+        self.add_own(here.chip)
         self.link("x_near").wait_recv()
         self.link("y_on").wait_recv()
         add_rows(self.acc, mine, ((self.acc, mine), (self.rx.at[0], 0), (self.r2.at[0], 0)), self.half)
@@ -1087,9 +1140,8 @@
         red = self.result()
         self.link("share").wait_recv()
         pltpu.make_async_copy(self.fin, red, local_sem).wait()
-        for name in ("core", "x_far", "x_near", "y_far", "y_near", "y_on", "x_on", "z_half", "z_far", "share"):
-            if name != "core" or self.first >= EARLY + MIDDLE:
-                self.link(name).wait_send()
+        for name in ("x_far", "x_near", "y_far", "y_near", "y_on", "x_on", "z_half", "z_far", "share"):
+            self.link(name).wait_send()
 
 
 def back_pair(q_ref, k_ref, v_ref, ctx_ref, do_ref, lse_ref, seq, p, bias):
@@ -1157,7 +1209,7 @@
         local(tok_in, tok, 7),
         local(w_in, w, 10),
     )
-    for load in first_loads:
+    for load in first_loads[:5]:
         load.start()
     here.meet()
 
@@ -1178,11 +1230,11 @@
         load.wait()
 
     early, middle = (
-        Reduce(here, sender, 24 + 11 * i, count // 2, first, 0, blk_ref, grad, pack, phase_buffers[i], red)
+        Reduce(here, sender, 24 + 14 * i, count // 2, first, 0, blk_ref, grad, pack, phase_buffers[i], red)
         for i, (count, first) in enumerate(((EARLY, 0), (MIDDLE, EARLY)))
     )
     late = [
-        Reduce(here, sender, 46 + 11 * i, LATE // 2, EARLY + MIDDLE, i * wide, blk_ref, grad, pack, phase_buffers[2 + i], red)
+        Reduce(here, sender, 52 + 14 * i, LATE // 2, EARLY + MIDDLE, i * wide, blk_ref, grad, pack, phase_buffers[2 + i], red)
         for i in range(2)
     ]
 
@@ -1207,10 +1259,11 @@
 
         @pl.when(step == CHUNKS + 2)
         def _():
-            early.start_plane()
+            early.start_far()
 
         @pl.when(step == CHUNKS + 3)
         def _():
+            early.start_near()
             for copy in swaps[0]:
                 copy.wait_send()
             for copy in swaps[1]:
@@ -1218,12 +1271,14 @@
 
         return 0
 
+    for load in first_loads[5:]:
+        load.start()
     grad[0:HEAD_BLOCKS] = jnp.zeros((HEAD_BLOCKS, BLK, D), jnp.bfloat16)
     lax.fori_loop(0, 1 + 2 * CHUNKS, grads, 0)
     more_loads = (local(v_in, att.at[2], 0), local(ctx_in, att.at[3], 1))
     for load in more_loads:
         load.start()
-    early.link("core").wait_send()
+    early.sent_core()
     middle.start_core()
     for load in first_loads[5:] + tuple(own_swaps) + more_loads:
         load.wait()
@@ -1240,7 +1295,7 @@
 
     def send_ingrad(s, hop):
         return sender.copy(
-            68 + 3 * s + hop,
+            80 + 3 * s + hop,
             att.at[0, pl.ds(s * rows + part * here.z_hops[hop], part)],
             ingrad.at[own * z + s],
             here.to_z[hop],
@@ -1259,6 +1314,10 @@
             send_ingrad(s, hop).start()
         own_ingrad(s).start()
 
+    def second_half():
+        for copy in swaps[1]:
+            copy.wait_recv()
+
     group = PAIRS // 2
 
     def pair_step(i, _):
@@ -1271,40 +1330,25 @@
         d3[2, at, cols] = d_key
         d3[0, at, cols] = d_value
 
-        @pl.when(i == 0)
-        def _():
-            early.pass_plane()
-
-        @pl.when(i == 2)
-        def _():
-            middle.start_plane()
-
-        @pl.when(i == 4)
-        def _():
-            early.start_z()
-
-        @pl.when(i == 5)
-        def _():
-            head_grads(0)
-            middle.link("core").wait_send()
-            late[0].start_core()
-            for copy in swaps[1]:
-                copy.wait_recv()
-
-        @pl.when(i == 6)
-        def _():
-            middle.pass_plane()
-            early.far_z()
-
-        @pl.when(i == 8)
-        def _():
-            late[0].start_plane()
-            input_gradient(0)
-
-        @pl.when(i == 11)
-        def _():
-            middle.start_z()
-            early.back_z()
+        stages = {
+            0: (early.pass_plane,),
+            2: (middle.start_far,),
+            3: (middle.start_near,),
+            4: (early.start_z,),
+            5: (lambda: head_grads(0), middle.sent_core, late[0].start_core, second_half),
+            6: (early.far_z,),
+            7: (middle.pass_plane,),
+            8: (late[0].start_far, lambda: input_gradient(0)),
+            9: (late[0].start_near,),
+            10: (early.back_z,),
+            11: (middle.start_z,),
+        }
+        for at_step, calls in stages.items():
+
+            @pl.when(i == at_step)
+            def _():
+                for call in calls:
+                    call()
 
         return 0
 
@@ -1350,8 +1394,9 @@
 
     late[0].pass_plane()
     vec_step(0)
-    late[1].start_plane()
+    late[1].start_far()
     middle.far_z()
+    late[1].start_near()
     input_gradient(1)
     vec_step(1)
     late[1].pass_plane()
@@ -1370,6 +1415,8 @@
     vec_step(5)
     late[1].back_z()
     late[1].share(load_sem.at[16])
+    for phase in late:
+        phase.sent_core()
     for i, phase in enumerate((early, middle, late[0], late[1])):
         phase.finish(load_sem.at[13 + i])
     for copy in swaps[1] + vec_copies + rms_copies:
@@ -1428,8 +1475,8 @@
             pltpu.VMEM((5,) + vec.shape, jnp.float32),
             pltpu.VMEM((2,) + sums, jnp.float32),
             pltpu.VMEM((2,) + sums, jnp.float32),
-            pltpu.SemaphoreType.DMA((74,)),
-            pltpu.SemaphoreType.DMA((74,)),
+            pltpu.SemaphoreType.DMA((86,)),
+            pltpu.SemaphoreType.DMA((86,)),
             pltpu.SemaphoreType.DMA((17,)),
         ],
         compiler_params=pltpu.CompilerParams(

time: 358 us -> 356 us (level)
  Pallas kernels: 335 us -> 331 us
    pallas_call x1, Pallas kernels: 95.7 us -> 92 us  [front(): pl.pallas_call(front_kernel, in_specs=[smem] * 3 + [vmem] + [any_spec] *...]
where the time goes in v2:
time: 356 us; the launch traced here: 351 us
  Pallas kernels  331 us (93%)
  between operations  15.1 us (4%)
  loops' own time  3.71 us (1%)
    pallas_call x1, Pallas kernels, tail(): pl.pallas_call(tail_kernel, in_specs=[smem] * 2 + [vmem] * 3 + [any_spec]...  164 us
    pallas_call x1, Pallas kernels, front(): pl.pallas_call(front_kernel, in_specs=[smem] * 3 + [vmem] + [any_spec] *...  92 us
    pallas_call x1, Pallas kernels, feed_both(): pl.pallas_call(partial(feed_kernel, seq_rows=seq_rows), grid_spec=pltpu.P...  46.1 us
    pallas_call x1, Pallas kernels, adam_all(): pl.pallas_call(adam_kernel, grid_spec=pltpu.PrefetchScalarGridSpec(num_sc...  25 us

profile of v2, /device:TPU:0, one launch (start us, length us, event | category | flops | bytes accessed | tf_op | source)
XLA Modules:
  0.0 350.9 jit_solution(15321497950174562140)
XLA Ops:
  7.2 3.6 %tables.1 = (s32[72]{0:T(128)}, s32[24]{0:T(128)}, s32[96]{0:T(128)}, s32[18]{0:T(128)}, s32[18]{0:T(128)}, /*index=5*/s32[1]{0:T(128)}) custom-call(s32[72]{0:T(128)} %owner_ref.1), custom_call_target="tpu_custom_call" | custom-call | tf_op jit(solution)/shard_map/tables/pallas_call | solution.py:1550
  11.4 305.8 %conditional.1 = (bf16[8,128,768]{2,1,0:T(8,128)(2,1)}, f32[1024,768]{1,0:T(8,128)}, bf16[1024,768]{1,0:T(8,128)(2,1)}, f32[8,128,768]{2,1,0:T(8,128)}, f32[16,7...) conditional(s32[]{:T(128)} %bitcast.58, (s32[8]{0:T(128)}, ...), branch_computations={%region_0.7_spmd, %region_6.8_spmd} | conditional | flops 49143767040 | bytes 522735680 | solution.py:1644
  14.8 0.0 copy-start.10
  14.8 0.0 copy-start.18
  14.8 0.0 copy-start.25
  14.8 0.0 copy-start.26
  14.9 92.0 %front.1 = (bf16[12288,768]{1,0:T(8,128)(2,1)}, bf16[1024,768]{1,0:T(8,128)(2,1)}, bf16[1024,768]{1,0:T(8,128)(2,1)}, bf16[1024,768]{1,0:T(8,128)(2,1)}, bf16[10...) custom-call(s32[72]{0:T(128)} %get-tuple-element.57.place_ref, ...), custom_call_target="tpu_custom_call" | custom-call | flops 5234491392 | bytes 45613056 | tf_op jit(solution)/shard_map/cond/branch_1_fun/front/pallas_call | solution.py:946
  106.9 0.0 copy-done.10
  106.9 0.0 copy-done.18
  106.9 0.0 copy-done.25
  106.9 0.0 copy-done.26
  106.9 0.0 copy-start.27
  106.9 46.1 %feed_both.3 = (f32[1024,768]{1,0:T(8,128)}, bf16[1024,768]{1,0:T(8,128)(2,1)}, bf16[1024,768]{1,0:T(8,128)(2,1)}, bf16[1024,3072]{1,0:T(8,128)(2,1)}, bf16[1024...) custom-call(s32[72]{0:T(128)S(1)} %copy-done.26, ...), custom_call_target="tpu_custom_call" | custom-call | flops 21743271936 | bytes 53477376 | tf_op jit(solution)/shard_map/cond/branch_1_fun/feed_both/pallas_call | solution.py:363
  153.1 0.0 copy-done.27
  153.1 163.9 %tail.1 = (bf16[3072,768]{1,0:T(8,128)(2,1)}, bf16[8,128,768]{2,1,0:T(8,128)(2,1)}, f32[16,768]{1,0:T(8,128)}, f32[8,128]{1,0:T(8,128)S(1)}) custom-call(s32[96]{0:T(128)S(1)} %copy-done.27, s32[8]{0:T(128)S(1)} %copy-done.25, f32[16,768]{1,0:T(8,128)} %get-tuple-element.69.vec_in, f32[2,8,768]{2,1,0:T(8,128)} %get-tuple-element.70.squares_in, ...), custom_call_target="tpu_custom_call" | custom-call | flops 20937965568 | bytes 50331648 | tf_op jit(solution)/shard_map/cond/branch_1_fun/tail/pallas_call | solution.py:1451
  317.3 25.0 %adam_all.1 = (f32[1024,768]{1,0:T(8,128)}, f32[8,2]{1,0:T(8,128)}, f32[18,128,768]{2,1,0:T(8,128)}, f32[18,128,768]{2,1,0:T(8,128)}, f32[18,128,768]{2,1,0:T(8,...) custom-call(s32[18]{0:T(128)} %get-tuple-element.135.place_ref, ...), custom_call_target="tpu_custom_call" | custom-call | flops 35389440 | bytes 53084160 | tf_op jit(solution)/shard_map/adam_all/pallas_call | solution.py:603
  342.3 1.3 copy.44
Async XLA Ops:
  14.8 92.1 %copy-start.10 = (bf16[8,128,768]{2,1,0:T(8,128)(2,1)S(1)}, bf16[8,128,768]{2,1,0:T(8,128)(2,1)}, u32[]{:S(2)}) copy-start(bf16[8,128,768]{2,1,0:T(8,128)(2,1)} %get-tuple-element.59.tokens_in) | copy-start | bytes 4718596 | tf_op jit(solution)/shard_map/cond
  14.8 92.1 %copy-start.18 = (f32[12,768]{1,0:T(8,128)S(1)}, f32[12,768]{1,0:T(8,128)}, u32[]{:S(2)}) copy-start(f32[12,768]{1,0:T(8,128)} %get-tuple-element.61.vec_ref) | copy-start | bytes 110596 | tf_op jit(solution)/shard_map/cond
  14.8 92.1 %copy-start.25 = (s32[8]{0:T(128)S(1)}, s32[8]{0:T(128)}, u32[]{:S(2)}) copy-start(s32[8]{0:T(128)} %get-tuple-element.58.lengths_ref) | copy-start | bytes 100 | tf_op jit(solution)/shard_map/cond
  14.8 92.1 %copy-start.26 = (s32[72]{0:T(128)S(1)}, s32[72]{0:T(128)}, u32[]{:S(2)}) copy-start(s32[72]{0:T(128)} %get-tuple-element.57.place_ref) | copy-start | bytes 868 | tf_op jit(solution)/shard_map/cond
  106.9 46.2 %copy-start.27 = (s32[96]{0:T(128)S(1)}, s32[96]{0:T(128)}, u32[]{:S(2)}) copy-start(s32[96]{0:T(128)} %get-tuple-element.68.blk_ref) | copy-start | bytes 1156 | tf_op jit(solution)/shard_map/cond

commit v3 on v2

--- a/solution.py
+++ b/solution.py
@@ -220,18 +220,17 @@
 
 
 def gelu_parts(x):
-    z = jnp.abs(x) * 0.7071067811865476
-    t_in = 1.0 + 0.3275911 * z
+    t_in = 1.0 + (0.3275911 * 0.7071067811865476) * jnp.abs(x)
     t = pltpu.reciprocal(t_in, approx=True)
     t = t * (2.0 - t_in * t)
-    e = jnp.exp(-0.5 * (x * x))
-    poly = 1.061405429 * t - 1.453152027
-    poly = poly * t + 1.421413741
-    poly = poly * t - 0.284496736
-    poly = poly * t + 0.254829592
-    tail = (0.5 * t) * poly * e
+    e = jnp.exp2((-0.5 * 1.4426950408889634) * (x * x))
+    poly = (0.5 * 1.061405429) * t - (0.5 * 1.453152027)
+    poly = poly * t + (0.5 * 1.421413741)
+    poly = poly * t - (0.5 * 0.284496736)
+    poly = poly * t + (0.5 * 0.254829592)
+    tail = (poly * t) * e
     dist = jnp.where(x >= 0, 1.0 - tail, tail)
-    return dist, x * e * 0.3989422804014327
+    return dist, x * (e * 0.3989422804014327)
 
 
 def norm_stats(resid):
@@ -297,31 +296,31 @@
     def _():
         wait_whole(w_up, sem.at[1])
 
-    feed = jnp.zeros((rows, D), jnp.float32) + vec_ref[3:4, :]
-    parts = [slice(c * D, (c + 1) * D) for c in range(CHUNKS)]
+    width = D // 2
+    count = FF // width
+    parts = [slice(c * width, (c + 1) * width) for c in range(count)]
+
+    def vec_part(c):
+        return (slice(8 + c // 2, 9 + c // 2), slice((c % 2) * width, (c % 2 + 1) * width))
 
     def up(c):
         return mm_nt(mid_low, w_up[parts[c], :])
 
     def bend(c, inner):
-        inner = inner + vec_ref[8 + c : 9 + c, :]
+        inner = inner + vec_ref[vec_part(c)]
         dist, bell = gelu_parts(inner)
         act = (inner * dist).astype(jnp.bfloat16)
         act_ref[:, parts[c]] = act
         slope_scr[:, parts[c]] = dist + bell
-        return act
-
-    inner = up(0)
+
+    for c in range(count):
+        bend(c, up(c))
 
     @pl.when(step == 0)
     def _():
         wait_whole(w_down, sem.at[2])
 
-    for c in range(CHUNKS):
-        after = up(c + 1) if c + 1 < CHUNKS else None
-        act = bend(c, inner)
-        feed += mm(act, w_down[parts[c], :])
-        inner = after
+    feed = mm(act_ref[...], w_down[...]) + vec_ref[3:4, :]
     square_sums(1, feed)
     hat2, scale2 = norm_stats(middle + feed)
     gain2 = vec_ref[6:7, :]
@@ -334,14 +333,11 @@
     dfeed_ref[...] = d_feed
     add_row(3, d_feed.astype(jnp.float32))
     d_mid = d_res2
-    d_act = mm_nt(d_feed, w_down[parts[0], :])
-    for c in range(CHUNKS):
-        after = mm_nt(d_feed, w_down[parts[c + 1], :]) if c + 1 < CHUNKS else None
-        d_inner = (d_act * slope_scr[:, parts[c]]).astype(jnp.bfloat16)
+    for c in range(count):
+        d_inner = (mm_nt(d_feed, w_down[parts[c], :]) * slope_scr[:, parts[c]]).astype(jnp.bfloat16)
         dinner_ref[:, parts[c]] = d_inner
-        add_row(8 + c, d_inner.astype(jnp.float32))
-        d_mid += mm(d_inner, w_up[parts[c], :])
-        d_act = after
+        grad_ref[vec_part(c)] += jnp.sum(d_inner.astype(jnp.float32), axis=0, keepdims=True)
+    d_mid = d_res2 + mm(dinner_ref[...], w_up[...])
     add_row(4, d_mid * hat1)
     add_row(5, d_mid)
     d_res1 = norm_back(d_mid, vec_ref[4:5, :], hat1, scale1)
@@ -352,7 +348,7 @@
     dctx_ref[...] = mm_nt(d_branch, w_out[...]).astype(jnp.bfloat16)
 
 
-def feed_both(place, lengths, seq_rows, tokens, ctx, cot, pool, vec, tile=512):
+def feed_both(place, lengths, seq_rows, tokens, ctx, cot, pool, vec, tile=256):
     total = tokens.shape[0]
     steps = total // tile
     row_spec = pl.BlockSpec((tile, D), lambda s, *_: (s, 0))
@@ -560,15 +556,16 @@
 
 
 def adam_kernel(
-    place_ref, has_ref, grad_a, grad_b, moment_ref, second_ref, master_ref,
-    dres_ref, part_ref, rms_ref, vec_ref, vec_moment_ref, vec_second_ref, vec_master_ref,
-    ingrad_out, rms_out, grad_out, moment_out, second_out, master_out,
-    vec_out, vec_moment_out, vec_second_out, vec_master_out,
+    place_ref, has_ref, *refs, per
 ):
+    moment_ref, second_ref, master_ref, dres_ref, part_ref, rms_ref, vec_ref = refs[per : per + 7]
+    vec_moment_ref, vec_second_ref, vec_master_ref = refs[per + 7 : per + 10]
+    ingrad_out, rms_out, grad_out, moment_out, second_out, master_out = refs[per + 10 : per + 16]
+    vec_out, vec_moment_out, vec_second_out, vec_master_out = refs[per + 16 :]
     step = pl.program_id(0)
-    for j, grad_in in enumerate((grad_a, grad_b)):
+    for j, grad_in in enumerate(refs[:per]):
         got = grad_in[0].astype(jnp.float32)
-        gradient = jnp.where(has_ref[2 * step + j] > 0, got, jnp.zeros_like(got))
+        gradient = jnp.where(has_ref[per * step + j] > 0, got, jnp.zeros_like(got))
         grad_out[j] = gradient
         moment_out[j], second_out[j], master_out[j] = adam_step(
             gradient, moment_ref[j], second_ref[j], master_ref[j], matrix_rate
@@ -587,12 +584,13 @@
 
 def adam_all(place, has, reduced, moment, second, master, d_res, part, rms, vec, vec_moment, vec_second, vec_master):
     slots = master.shape[0]
-    steps = slots // 2
+    per = 3 if slots % 3 == 0 else 2
+    steps = slots // per
     total = d_res.shape[0]
     pieces = 1
     while 2 * pieces <= steps:
         pieces *= 2
-    pair = pl.BlockSpec((2, BLK, D), lambda s, *_: (s, 0, 0))
+    some = pl.BlockSpec((per, BLK, D), lambda s, *_: (s, 0, 0))
     rows = pl.BlockSpec((total // pieces, D), lambda s, *_: (jnp.minimum(s, pieces - 1), 0))
 
     def whole(shape):
@@ -601,19 +599,19 @@
     full = jax.ShapeDtypeStruct(master.shape, jnp.float32)
     vec_full = jax.ShapeDtypeStruct(vec_master.shape, jnp.float32)
     return pl.pallas_call(
-        adam_kernel,
+        partial(adam_kernel, per=per),
         grid_spec=pltpu.PrefetchScalarGridSpec(
             num_scalar_prefetch=2,
             grid=(steps,),
             in_specs=[
-                pl.BlockSpec((1, BLK, D), lambda s, place, has: (place[2 * s], 0, 0)),
-                pl.BlockSpec((1, BLK, D), lambda s, place, has: (place[2 * s + 1], 0, 0)),
+                pl.BlockSpec((1, BLK, D), partial(lambda j, s, place, has: (place[per * s + j], 0, 0), j))
+                for j in range(per)
             ]
-            + [pair] * 3
+            + [some] * 3
             + [rows] * 2
             + [whole(rms.shape), whole(vec.shape)]
             + [whole(vec_master.shape)] * 3,
-            out_specs=[rows, whole((rms.shape[0], 2))] + [pair] * 4 + [whole(vec_master.shape)] * 4,
+            out_specs=[rows, whole((rms.shape[0], 2))] + [some] * 4 + [whole(vec_master.shape)] * 4,
         ),
         out_shape=[
             jax.ShapeDtypeStruct(d_res.shape, jnp.float32),
@@ -626,7 +624,7 @@
             flops=20 * slots * BLK * D, bytes_accessed=30 * slots * BLK * D, transcendentals=2 * slots * BLK * D
         ),
         name="adam_all",
-    )(place, has, reduced, reduced, moment, second, master, d_res, part, rms, vec, vec_moment, vec_second, vec_master)
+    )(place, has, *(reduced,) * per, moment, second, master, d_res, part, rms, vec, vec_moment, vec_second, vec_master)
 
 
 EARLY = 6
@@ -1257,17 +1255,20 @@
         def _():
             early.start_core()
 
-        @pl.when(step == CHUNKS + 2)
+        @pl.when(step == CHUNKS + 1)
         def _():
-            early.start_far()
-
-        @pl.when(step == CHUNKS + 3)
-        def _():
-            early.start_near()
             for copy in swaps[0]:
                 copy.wait_send()
             for copy in swaps[1]:
                 copy.start()
+
+        @pl.when(step == CHUNKS + 2)
+        def _():
+            early.start_far()
+
+        @pl.when(step == CHUNKS + 3)
+        def _():
+            early.start_near()
 
         return 0
 
@@ -1333,15 +1334,13 @@
         stages = {
             0: (early.pass_plane,),
             2: (middle.start_far,),
-            3: (middle.start_near,),
-            4: (early.start_z,),
-            5: (lambda: head_grads(0), middle.sent_core, late[0].start_core, second_half),
-            6: (early.far_z,),
-            7: (middle.pass_plane,),
-            8: (late[0].start_far, lambda: input_gradient(0)),
-            9: (late[0].start_near,),
-            10: (early.back_z,),
-            11: (middle.start_z,),
+            4: (early.start_z, middle.start_near),
+            5: (lambda: head_grads(0), second_half),
+            6: (early.far_z, middle.pass_plane),
+            8: (lambda: input_gradient(0),),
+            9: (middle.sent_core, late[0].start_core, middle.start_z, late[0].start_far),
+            10: (late[0].start_near,),
+            11: (late[0].pass_plane,),
         }
         for at_step, calls in stages.items():
 
@@ -1392,28 +1391,28 @@
         if w < 2:
             rms_copies[w].start()
 
-    late[0].pass_plane()
     vec_step(0)
     late[1].start_far()
+    early.back_z()
     middle.far_z()
+    vec_step(1)
+    late[0].start_z()
     late[1].start_near()
+    late[1].pass_plane()
+    vec_step(2)
+    late[1].start_z()
+    early.share(load_sem.at[13])
+    vec_step(3)
+    late[0].far_z()
+    middle.back_z()
+    vec_step(4)
+    late[1].far_z()
     input_gradient(1)
-    vec_step(1)
-    late[1].pass_plane()
-    late[0].start_z()
-    early.share(load_sem.at[13])
-    vec_step(2)
-    late[0].far_z()
-    late[1].start_z()
-    vec_step(3)
-    late[1].far_z()
-    middle.back_z()
+    vec_step(5)
     late[0].back_z()
-    vec_step(4)
+    late[1].back_z()
+    late[0].share(load_sem.at[15])
     middle.share(load_sem.at[14])
-    late[0].share(load_sem.at[15])
-    vec_step(5)
-    late[1].back_z()
     late[1].share(load_sem.at[16])
     for phase in late:
         phase.sent_core()

time: 356 us -> 351 us (0.986)
  Pallas kernels: 331 us -> 326 us
    pallas_call x1, Pallas kernels: 164 us -> 160 us  [tail(): pl.pallas_call(tail_kernel, in_specs=[smem] * 2 + [vmem] * 3 + [any_spec]...]
where the time goes in v3:
time: 351 us; the launch traced here: 346 us
  Pallas kernels  326 us (93%)
  between operations  14.9 us (4%)
    pallas_call x1, Pallas kernels, tail(): pl.pallas_call(tail_kernel, in_specs=[smem] * 2 + [vmem] * 3 + [any_spec]...  160 us
    pallas_call x1, Pallas kernels, front(): pl.pallas_call(front_kernel, in_specs=[smem] * 3 + [vmem] + [any_spec] *...  92 us
    pallas_call x1, Pallas kernels, feed_both(): pl.pallas_call(partial(feed_kernel, seq_rows=seq_rows), grid_spec=pltpu.P...  47.6 us
    pallas_call x1, Pallas kernels, adam_all(): pl.pallas_call(partial(adam_kernel, per=per), grid_spec=pltpu.PrefetchSca...  22.8 us

profile of v3, /device:TPU:0, one launch (start us, length us, event | category | flops | bytes accessed | tf_op | source)
XLA Modules:
  0.0 346.0 jit_solution(18156822386466921368)
XLA Ops:
  7.2 3.6 %tables.1 = (s32[72]{0:T(128)}, s32[24]{0:T(128)}, s32[96]{0:T(128)}, s32[18]{0:T(128)}, s32[18]{0:T(128)}, /*index=5*/s32[1]{0:T(128)}) custom-call(s32[72]{0:T(128)} %owner_ref.1), custom_call_target="tpu_custom_call" | custom-call | tf_op jit(solution)/shard_map/tables/pallas_call | solution.py:1549
  11.4 303.3 %conditional.1 = (bf16[8,128,768]{2,1,0:T(8,128)(2,1)}, f32[1024,768]{1,0:T(8,128)}, bf16[1024,768]{1,0:T(8,128)(2,1)}, f32[8,128,768]{2,1,0:T(8,128)}, f32[16,7...) conditional(s32[]{:T(128)} %bitcast.58, (s32[8]{0:T(128)}, ...), branch_computations={%region_0.7_spmd, %region_6.8_spmd} | conditional | flops 49143767040 | bytes 522747968 | solution.py:1643
  14.6 0.0 copy-start.10
  14.6 0.0 copy-start.18
  14.6 0.0 copy-start.25
  14.6 0.0 copy-start.26
  14.7 92.0 %front.1 = (bf16[12288,768]{1,0:T(8,128)(2,1)}, bf16[1024,768]{1,0:T(8,128)(2,1)}, bf16[1024,768]{1,0:T(8,128)(2,1)}, bf16[1024,768]{1,0:T(8,128)(2,1)}, bf16[10...) custom-call(s32[72]{0:T(128)} %get-tuple-element.57.place_ref, ...), custom_call_target="tpu_custom_call" | custom-call | flops 5234491392 | bytes 45613056 | tf_op jit(solution)/shard_map/cond/branch_1_fun/front/pallas_call | solution.py:944
  106.7 0.0 copy-done.10
  106.7 0.0 copy-done.18
  106.7 0.0 copy-done.25
  106.7 0.0 copy-done.26
  106.7 0.0 copy-start.27
  106.7 47.6 %feed_both.3 = (f32[1024,768]{1,0:T(8,128)}, bf16[1024,768]{1,0:T(8,128)(2,1)}, bf16[1024,768]{1,0:T(8,128)(2,1)}, bf16[1024,3072]{1,0:T(8,128)(2,1)}, bf16[1024...) custom-call(s32[72]{0:T(128)S(1)} %copy-done.26, ...), custom_call_target="tpu_custom_call" | custom-call | flops 21743271936 | bytes 53477376 | tf_op jit(solution)/shard_map/cond/branch_1_fun/feed_both/pallas_call | solution.py:359
  154.4 0.0 copy-done.27
  154.4 160.2 %tail.1 = (bf16[3072,768]{1,0:T(8,128)(2,1)}, bf16[8,128,768]{2,1,0:T(8,128)(2,1)}, f32[16,768]{1,0:T(8,128)}, f32[8,128]{1,0:T(8,128)S(1)}) custom-call(s32[96]{0:T(128)S(1)} %copy-done.27, s32[8]{0:T(128)S(1)} %copy-done.25, f32[16,768]{1,0:T(8,128)} %get-tuple-element.69.vec_in, f32[4,8,768]{2,1,0:T(8,128)} %get-tuple-element.70.squares_in, ...), custom_call_target="tpu_custom_call" | custom-call | flops 20937965568 | bytes 50331648 | tf_op jit(solution)/shard_map/cond/branch_1_fun/tail/pallas_call | solution.py:1450
  314.8 22.8 %adam_all.1 = (f32[1024,768]{1,0:T(8,128)}, f32[8,2]{1,0:T(8,128)}, f32[18,128,768]{2,1,0:T(8,128)}, f32[18,128,768]{2,1,0:T(8,128)}, f32[18,128,768]{2,1,0:T(8,...) custom-call(s32[18]{0:T(128)} %get-tuple-element.135.place_ref, ...), custom_call_target="tpu_custom_call" | custom-call | flops 35389440 | bytes 53084160 | tf_op jit(solution)/shard_map/adam_all/pallas_call | solution.py:601
  337.6 1.3 copy.44
Async XLA Ops:
  14.6 92.1 %copy-start.10 = (bf16[8,128,768]{2,1,0:T(8,128)(2,1)S(1)}, bf16[8,128,768]{2,1,0:T(8,128)(2,1)}, u32[]{:S(2)}) copy-start(bf16[8,128,768]{2,1,0:T(8,128)(2,1)} %get-tuple-element.59.tokens_in) | copy-start | bytes 4718596 | tf_op jit(solution)/shard_map/cond
  14.6 92.1 %copy-start.18 = (f32[12,768]{1,0:T(8,128)S(1)}, f32[12,768]{1,0:T(8,128)}, u32[]{:S(2)}) copy-start(f32[12,768]{1,0:T(8,128)} %get-tuple-element.61.vec_ref) | copy-start | bytes 110596 | tf_op jit(solution)/shard_map/cond
  14.6 92.1 %copy-start.25 = (s32[8]{0:T(128)S(1)}, s32[8]{0:T(128)}, u32[]{:S(2)}) copy-start(s32[8]{0:T(128)} %get-tuple-element.58.lengths_ref) | copy-start | bytes 100 | tf_op jit(solution)/shard_map/cond
  14.6 92.1 %copy-start.26 = (s32[72]{0:T(128)S(1)}, s32[72]{0:T(128)}, u32[]{:S(2)}) copy-start(s32[72]{0:T(128)} %get-tuple-element.57.place_ref) | copy-start | bytes 868 | tf_op jit(solution)/shard_map/cond
  106.7 47.7 %copy-start.27 = (s32[96]{0:T(128)S(1)}, s32[96]{0:T(128)}, u32[]{:S(2)}) copy-start(s32[96]{0:T(128)} %get-tuple-element.68.blk_ref) | copy-start | bytes 1156 | tf_op jit(solution)/shard_map/cond
